TPU v7x, 32 devices: a whole 2x2x4 slice. The times are simulated.
32 devices in a mesh: dp: 4 (over y, x), expert: 8 (over z, core).
Axes of the slice: x: 2, y: 2, z: 4, core: 2. Of those that a mesh axis runs over, the one named last changes fastest.
Arguments:
- activations: bfloat16 [4, 1024, 1024], P('dp', 'expert'), may hold values from -6 to 6
- doc_ids: int32 [4, 1024], P('dp', 'expert'), may hold values from 0 to 3, never falling along the last dimension, each value on 1 to 512 neighbouring positions
- routes: int32 [4, 1024, 8], P('dp', 'expert'), may hold values from 0 to 15, all different within a row; in each aligned block of 128 rows (0 to 127, 128 to 255, ..., all dimensions but the last counted through in order) at most 72 rows name the same one
- gate_weights: float32 [4, 1024, 8], P('dp', 'expert'), may hold values from 0.07 to 0.2
- cotangent: bfloat16 [4, 1024, 1024], P('dp', 'expert'), may hold values from -6 to 6
- step_count: int32 [], replicated, may hold values from 1 to 20
- w_attn: float32 [1024, 3072], P(('dp', 'expert'))
- norm_gains: float32 [1024, 2], P(('dp', 'expert'))
- w_expert: float32 [16, 1024, 1536], P('expert', 'dp')
- first_attn: float32 [1024, 3072], P(('dp', 'expert')), may hold values from -0.00030517578 to 0.00030517578
- second_attn: float32 [1024, 3072], P(('dp', 'expert')), may hold values from 1.7659358e-09 to 7.0637434e-09
- first_gains: float32 [1024, 2], P(('dp', 'expert')), may hold values from -0.0012207031 to 0.0012207031
- second_gains: float32 [1024, 2], P(('dp', 'expert')), may hold values from 2.8254973e-08 to 1.13019894e-07
- first_expert: float32 [16, 1024, 1536], P('expert', 'dp'), may hold values from -0.00030517578 to 0.00030517578
- second_expert: float32 [16, 1024, 1536], P('expert', 'dp'), may hold values from 1.7659358e-09 to 7.0637434e-09
Outputs:
- block_out: bfloat16 [4, 1024, 1024], P('dp', 'expert')
- input_grad: float32 [4, 1024, 1024], P('dp', 'expert')
- grad_norm: float32 [], replicated
- new_attn: float32 [1024, 3072], P(('dp', 'expert'))
- new_first_attn: float32 [1024, 3072], P(('dp', 'expert'))
- new_second_attn: float32 [1024, 3072], P(('dp', 'expert'))
- new_gains: float32 [1024, 2], P(('dp', 'expert'))
- new_first_gains: float32 [1024, 2], P(('dp', 'expert'))
- new_second_gains: float32 [1024, 2], P(('dp', 'expert'))
- new_expert: float32 [16, 1024, 1536], P('expert', 'dp')
- new_first_expert: float32 [16, 1024, 1536], P('expert', 'dp')
- new_second_expert: float32 [16, 1024, 1536], P('expert', 'dp')
Inputs may be any that keep to these rules, and one draw needn't show every extreme that they name: `routes`: each row names 8 different experts. In each aligned block of 128 rows (the rows of one device) no expert is named by more than 72 rows, a bound that some block reaches. `doc_ids`: document numbers never fall along a sequence; a document has 1 to 512 positions, and one has exactly 512.
All inputs are finite; a program needn't handle non-finite values.
Results may differ from a plain program's by a relative error of at most 0.015.
The roundings to bfloat16 on the way count: a program that leaves them out, or rounds other values in their place, can miss the bound.
Values may be sent and summed in bfloat16 or wider, within the bound.
A program may use at most 192 MiB of HBM per device.

v0:
```python
import jax
import jax.numpy as jnp
from jax import lax
from jax.sharding import PartitionSpec as P

D = 1024
H = 16
KVH = 8
HD = 64
FF = 512
TOP = 8
QD = 1024
KVD = 512
QKV = 2048


EPSILON = 1e-05
ROPE_BASE = 10000.0
CLIP_NORM = 1.0
BETA_ONE = 0.9
BETA_TWO = 0.95
ADAM_EPSILON = 1e-08
LEARN_RATE = 0.03
GAIN_RATE = 0.4
WEIGHT_DECAY = 0.1


def rms_scale(values, gain):
    return values * lax.rsqrt(jnp.mean(values * values, axis=-1, keepdims=True) + EPSILON) * gain


def rope_tables(positions, head_width):
    halves = jnp.arange(head_width // 2, dtype=jnp.float32)
    inverse = ROPE_BASE ** (-2.0 * halves / head_width)
    angles = positions.astype(jnp.float32)[:, None] * inverse[None, :]
    angles = jnp.concatenate([angles, angles], axis=-1)
    return (jnp.cos(angles)[:, None, :], jnp.sin(angles)[:, None, :])


def rotate(values, cosine, sine_table):
    middle = values.shape[-1] // 2
    turned = jnp.concatenate([-values[..., middle:], values[..., :middle]], axis=-1)
    return values * cosine + turned * sine_table


def unrotate(gradient, cosine, sine_table):
    middle = gradient.shape[-1] // 2
    product = gradient * sine_table
    turned = jnp.concatenate([product[..., middle:], -product[..., :middle]], axis=-1)
    return gradient * cosine + turned


def adam_update(weight, moment_one, second, gradient, steps_done, decay_rate, step_rate):
    first_new = BETA_ONE * moment_one + (1.0 - BETA_ONE) * gradient
    second_new = BETA_TWO * second + (1.0 - BETA_TWO) * gradient * gradient
    first_hat = first_new / (1.0 - BETA_ONE**steps_done)
    second_hat = second_new / (1.0 - BETA_TWO**steps_done)
    weight_new = weight - step_rate * (
        first_hat / (jnp.sqrt(second_hat) + ADAM_EPSILON) + decay_rate * weight
    )
    return (weight_new, first_new, second_new)


def attn_fetch(w_attn, norm_gains):
    return (
        lax.all_gather(w_attn.astype(jnp.bfloat16), ("dp", "expert"), axis=0, tiled=True),
        lax.all_gather(norm_gains.astype(jnp.bfloat16), ("dp", "expert"), axis=0, tiled=True),
    )


def expert_fetch(w_expert):
    return lax.all_gather(w_expert.astype(jnp.bfloat16), "dp", axis=1, tiled=True)


def to_owner(buffer):
    return lax.all_to_all(buffer, "expert", split_axis=0, concat_axis=1, tiled=True)


def to_sender(buffer):
    return lax.all_to_all(buffer, "expert", split_axis=1, concat_axis=0, tiled=True)


def expert_forward(received, expert_cols):
    gate_up = jnp.einsum(
        "esd,edf->esf", received, expert_cols[:, :, : 2 * FF], preferred_element_type=jnp.float32
    )
    activated = (jax.nn.silu(gate_up[..., :FF]) * gate_up[..., FF:]).astype(jnp.bfloat16)
    return (gate_up, activated)


def body(
    activations,
    doc_ids,
    routes,
    gate_weights,
    cotangent,
    step_count,
    w_attn,
    norm_gains,
    w_expert,
    first_attn,
    second_attn,
    first_gains,
    second_gains,
    first_expert,
    second_expert,
):
    row_count = activations.shape[1]
    span_size = lax.axis_size("expert")
    shard_pos = lax.axis_index("expert")
    seq_length = row_count * span_size
    expert_total = w_expert.shape[0] * span_size
    capacity = (row_count * TOP * 9 + expert_total * 8 - 1) // (expert_total * 8)
    group_size = H // KVH
    score_scale = HD ** (-0.5)
    hidden_in = activations[0].astype(jnp.float32)
    upstream = cotangent[0].astype(jnp.float32)
    attn_cols, gain_pair = attn_fetch(w_attn, norm_gains)
    expert_cols = expert_fetch(w_expert)
    gain_one = gain_pair[:, 0].astype(jnp.float32)
    gain_two = gain_pair[:, 1].astype(jnp.float32)
    w_project = attn_cols[:, :QKV]
    w_output = attn_cols[:, QKV:]
    normed = rms_scale(hidden_in, gain_one).astype(jnp.bfloat16)
    projected = jnp.dot(normed, w_project, preferred_element_type=jnp.float32)
    positions = shard_pos * row_count + jnp.arange(row_count, dtype=jnp.int32)
    cosine, sine_table = rope_tables(positions, HD)
    queries = rotate(projected[:, :QD].reshape(row_count, H, HD), cosine, sine_table).astype(
        jnp.bfloat16
    )
    key_heads = rotate(
        projected[:, QD : QD + KVD].reshape(row_count, KVH, HD), cosine, sine_table
    ).astype(jnp.bfloat16)
    value_heads = projected[:, QD + KVD :].astype(jnp.bfloat16)
    key_all, value_all, doc_all = (
        lax.all_gather(key_heads.reshape(row_count, KVD), "expert", axis=0, tiled=True),
        lax.all_gather(value_heads, "expert", axis=0, tiled=True),
        lax.all_gather(doc_ids[0].astype(jnp.bfloat16), "expert", axis=0, tiled=True),
    )
    key_docs = doc_all.astype(jnp.int32)
    query_docs = doc_ids[0]
    query_groups = queries.reshape(row_count, KVH, group_size, HD)
    key_block = min(512, seq_length)
    needed = (shard_pos * row_count + row_count + key_block - 1) // key_block

    def block_scores(block_id):
        first_key = block_id * key_block
        key_part = lax.dynamic_slice_in_dim(key_all, first_key, key_block, 0).reshape(
            key_block, KVH, HD
        )
        raw_scores = (
            jnp.einsum("tgrd,kgd->grtk", query_groups, key_part, preferred_element_type=jnp.float32)
            * score_scale
        )
        key_pos = first_key + jnp.arange(key_block, dtype=jnp.int32)
        key_doc = lax.dynamic_slice_in_dim(key_docs, first_key, key_block, 0)
        visible = (key_pos[None, :] <= positions[:, None]) & (
            key_doc[None, :] == query_docs[:, None]
        )
        return (raw_scores, visible, key_part)

    def value_part(block_id):
        return lax.dynamic_slice_in_dim(value_all, block_id * key_block, key_block, 0).reshape(
            key_block, KVH, HD
        )

    def total_step(block_id, running):
        row_peak, row_total = running
        raw_scores, visible, _ = block_scores(block_id)
        masked = jnp.where(visible, raw_scores, -1e30)
        new_peak = jnp.maximum(row_peak, jnp.max(masked, axis=-1))
        scaled = jnp.where(visible, jnp.exp(masked - new_peak[..., None]), 0.0)
        return (new_peak, row_total * jnp.exp(row_peak - new_peak) + jnp.sum(scaled, axis=-1))

    start_peak = jnp.full((KVH, group_size, row_count), -1e30, jnp.float32)
    start_total = jnp.zeros((KVH, group_size, row_count), jnp.float32)
    row_peak, row_total = lax.fori_loop(0, needed, total_step, (start_peak, start_total))
    log_total = row_peak + jnp.log(row_total)

    def exact_probs(raw_scores, visible):
        return jnp.exp(jnp.where(visible, raw_scores - log_total[..., None], -1e30))

    def output_step(block_id, summed):
        raw_scores, visible, _ = block_scores(block_id)
        weights_low = exact_probs(raw_scores, visible).astype(jnp.bfloat16)
        return summed + jnp.einsum(
            "grtk,kgd->tgrd", weights_low, value_part(block_id), preferred_element_type=jnp.float32
        )

    attended = lax.fori_loop(
        0, needed, output_step, jnp.zeros((row_count, KVH, group_size, HD), jnp.float32)
    )
    attended = attended.reshape(row_count, QD).astype(jnp.bfloat16)
    branch = jnp.einsum("tc,dc->td", attended, w_output, preferred_element_type=jnp.float32)
    residual = hidden_in + branch
    normed_two = rms_scale(residual, gain_two).astype(jnp.bfloat16)
    flat_routes = routes[0].reshape(-1)
    one_hot = (flat_routes[:, None] == jnp.arange(expert_total, dtype=jnp.int32)[None, :]).astype(
        jnp.int32
    )
    ranking = jnp.sum((jnp.cumsum(one_hot, axis=0) - 1) * one_hot, axis=1)
    places = flat_routes * capacity + ranking
    owners = jnp.arange(row_count * TOP, dtype=jnp.int32) // TOP
    source = jnp.zeros((expert_total * capacity,), jnp.int32).at[places].set(owners)
    filled = jnp.zeros((expert_total * capacity,), jnp.int32).at[places].set(1) > 0
    slot_gate = (
        jnp.zeros((expert_total * capacity,), jnp.float32)
        .at[places]
        .set(gate_weights[0].reshape(-1))
    )
    outgoing = jnp.where(filled[:, None], normed_two[source], jnp.zeros((), jnp.bfloat16)).reshape(
        expert_total, capacity, D
    )
    received = to_owner(outgoing)
    gate_up, activated = expert_forward(received, expert_cols)
    expert_out = jnp.einsum(
        "esf,edf->esd", activated, expert_cols[:, :, 2 * FF :], preferred_element_type=jnp.float32
    ).astype(jnp.bfloat16)
    returned = to_sender(expert_out).reshape(expert_total * capacity, D)
    picked = returned[places].reshape(row_count, TOP, D).astype(jnp.float32)
    combined = jnp.sum(gate_weights[0][..., None] * picked, axis=1)
    block_result = (residual + combined).astype(jnp.bfloat16)
    slot_grad = jnp.where(filled[:, None], slot_gate[:, None] * upstream[source], 0.0)
    slot_grad = slot_grad.astype(jnp.bfloat16).reshape(expert_total, capacity, D)
    owner_grad = to_owner(slot_grad)
    attn_cols, gain_pair = attn_fetch(w_attn, norm_gains)
    w_project = attn_cols[:, :QKV]
    w_output = attn_cols[:, QKV:]
    expert_cols = expert_fetch(w_expert)
    gate_up, activated = expert_forward(received, expert_cols)
    gate_part = gate_up[..., :FF]
    up_part = gate_up[..., FF:]
    sigmoid_gate = jax.nn.sigmoid(gate_part)
    act_grad = jnp.einsum(
        "esd,edf->esf", owner_grad, expert_cols[:, :, 2 * FF :], preferred_element_type=jnp.float32
    )
    gate_grad = act_grad * up_part * sigmoid_gate * (1.0 + gate_part * (1.0 - sigmoid_gate))
    lift_grad = act_grad * gate_part * sigmoid_gate
    mixed_grad = jnp.concatenate([gate_grad, lift_grad], axis=-1).astype(jnp.bfloat16)
    down_grad = jnp.einsum(
        "esf,esd->edf", activated, owner_grad, preferred_element_type=jnp.float32
    )
    inward_grad = jnp.einsum(
        "esd,esf->edf", received, mixed_grad, preferred_element_type=jnp.float32
    )
    row_grads = jnp.einsum(
        "esf,edf->esd", mixed_grad, expert_cols[:, :, : 2 * FF], preferred_element_type=jnp.float32
    ).astype(jnp.bfloat16)
    back_rows = to_sender(row_grads).reshape(expert_total * capacity, D)
    normed_two_grad = jnp.sum(
        back_rows[places].reshape(row_count, TOP, D).astype(jnp.float32), axis=1
    )
    _, second_pull = jax.vjp(rms_scale, residual, gain_two)
    resid_grad, gain_two_grad = second_pull(normed_two_grad)
    resid_grad = upstream + resid_grad
    branch_grad = resid_grad.astype(jnp.bfloat16)
    output_grad = jnp.einsum("td,tc->dc", branch_grad, attended, preferred_element_type=jnp.float32)
    attended_grad = jnp.dot(branch_grad, w_output, preferred_element_type=jnp.float32).astype(
        jnp.bfloat16
    )
    grad_groups = attended_grad.reshape(row_count, KVH, group_size, HD)

    def delta_step(block_id, summed):
        raw_scores, visible, _ = block_scores(block_id)
        probs_full = exact_probs(raw_scores, visible)
        prob_grad = jnp.einsum(
            "tgrd,kgd->grtk", grad_groups, value_part(block_id), preferred_element_type=jnp.float32
        )
        return summed + jnp.sum(probs_full * prob_grad, axis=-1)

    delta_rows = lax.fori_loop(
        0, needed, delta_step, jnp.zeros((KVH, group_size, row_count), jnp.float32)
    )

    def grad_step(block_id, running):
        query_grad, key_grad, value_grad = running
        raw_scores, visible, key_part = block_scores(block_id)
        probs_full = exact_probs(raw_scores, visible)
        prob_grad = jnp.einsum(
            "tgrd,kgd->grtk", grad_groups, value_part(block_id), preferred_element_type=jnp.float32
        )
        score_grad = (probs_full * (prob_grad - delta_rows[..., None])).astype(jnp.bfloat16)
        query_grad = (
            query_grad
            + jnp.einsum("grtk,kgd->tgrd", score_grad, key_part, preferred_element_type=jnp.float32)
            * score_scale
        )
        key_piece = (
            jnp.einsum(
                "grtk,tgrd->kgd", score_grad, query_groups, preferred_element_type=jnp.float32
            )
            * score_scale
        )
        value_piece = jnp.einsum(
            "grtk,tgrd->kgd",
            probs_full.astype(jnp.bfloat16),
            grad_groups,
            preferred_element_type=jnp.float32,
        )
        first_key = block_id * key_block
        key_grad = lax.dynamic_update_slice_in_dim(
            key_grad, key_piece.reshape(key_block, KVD), first_key, 0
        )
        value_grad = lax.dynamic_update_slice_in_dim(
            value_grad, value_piece.reshape(key_block, KVD), first_key, 0
        )
        return (query_grad, key_grad, value_grad)

    start_grads = (
        jnp.zeros((row_count, KVH, group_size, HD), jnp.float32),
        jnp.zeros((seq_length, KVD), jnp.float32),
        jnp.zeros((seq_length, KVD), jnp.float32),
    )
    query_grad, key_grad, value_grad = lax.fori_loop(0, needed, grad_step, start_grads)
    key_sum, value_sum = (
        lax.psum_scatter(key_grad, "expert", scatter_dimension=0, tiled=True),
        lax.psum_scatter(value_grad, "expert", scatter_dimension=0, tiled=True),
    )
    query_back = unrotate(query_grad.reshape(row_count, H, HD), cosine, sine_table).reshape(
        row_count, QD
    )
    key_back = unrotate(key_sum.reshape(row_count, KVH, HD), cosine, sine_table).reshape(
        row_count, KVD
    )
    project_grad = jnp.concatenate([query_back, key_back, value_sum], axis=1).astype(jnp.bfloat16)
    weight_grad_qkv = jnp.einsum(
        "td,tc->dc", normed, project_grad, preferred_element_type=jnp.float32
    )
    normed_grad = jnp.einsum(
        "tc,dc->td", project_grad, w_project, preferred_element_type=jnp.float32
    )
    _, first_pull = jax.vjp(rms_scale, hidden_in, gain_one)
    input_part, gain_one_grad = first_pull(normed_grad)
    input_total = resid_grad + input_part
    attn_partial = jnp.concatenate([weight_grad_qkv, output_grad], axis=1)
    gain_partial = jnp.stack([gain_one_grad, gain_two_grad], axis=1)
    grad_attn, grad_gains = (
        lax.psum_scatter(attn_partial, ("dp", "expert"), scatter_dimension=0, tiled=True),
        lax.psum_scatter(gain_partial, ("dp", "expert"), scatter_dimension=0, tiled=True),
    )
    grad_expert = lax.psum_scatter(
        jnp.concatenate([inward_grad, down_grad], axis=2).astype(jnp.bfloat16),
        "dp",
        scatter_dimension=1,
        tiled=True,
    ).astype(jnp.float32)
    local_squares = (
        jnp.sum(grad_attn * grad_attn)
        + jnp.sum(grad_gains * grad_gains)
        + jnp.sum(grad_expert * grad_expert)
    )
    grad_norm = jnp.sqrt(lax.psum(local_squares, ("dp", "expert")))
    clip_factor = jnp.minimum(1.0, CLIP_NORM / (grad_norm + 1e-06))
    steps_done = step_count.astype(jnp.float32)
    attn_new = adam_update(
        w_attn,
        first_attn,
        second_attn,
        grad_attn * clip_factor,
        steps_done,
        WEIGHT_DECAY,
        LEARN_RATE,
    )
    gains_new = adam_update(
        norm_gains, first_gains, second_gains, grad_gains * clip_factor, steps_done, 0.0, GAIN_RATE
    )
    expert_new = adam_update(
        w_expert,
        first_expert,
        second_expert,
        grad_expert * clip_factor,
        steps_done,
        WEIGHT_DECAY,
        LEARN_RATE,
    )
    return (
        block_result[None],
        input_total[None],
        grad_norm,
        attn_new[0],
        attn_new[1],
        attn_new[2],
        gains_new[0],
        gains_new[1],
        gains_new[2],
        expert_new[0],
        expert_new[1],
        expert_new[2],
    )


def solution(mesh):
    in_specs = (
        P("dp", "expert", None),
        P("dp", "expert"),
        P("dp", "expert", None),
        P("dp", "expert", None),
        P("dp", "expert", None),
        P(),
        P(("dp", "expert"), None),
        P(("dp", "expert"), None),
        P("expert", "dp", None),
        P(("dp", "expert"), None),
        P(("dp", "expert"), None),
        P(("dp", "expert"), None),
        P(("dp", "expert"), None),
        P("expert", "dp", None),
        P("expert", "dp", None),
    )
    out_specs = (
        P("dp", "expert", None),
        P("dp", "expert", None),
        P(),
        P(("dp", "expert"), None),
        P(("dp", "expert"), None),
        P(("dp", "expert"), None),
        P(("dp", "expert"), None),
        P(("dp", "expert"), None),
        P(("dp", "expert"), None),
        P("expert", "dp", None),
        P("expert", "dp", None),
        P("expert", "dp", None),
    )
    return jax.shard_map(body, mesh=mesh, in_specs=in_specs, out_specs=out_specs, check_vma=False)
```

profile of v0, /device:TPU:24, one launch (start us, length us, event | category | flops | bytes accessed | tf_op | source)
XLA Modules:
  0.0 977.2 jit_solution(13153232522634948539)
XLA Ops:
  9.7 32.2 %all-gather.1 = bf16[32,32,2]{1,2,0:T(2,128)(2,1)S(1)} all-gather(bf16[1,32,2]{1,2,0:T(2,128)(2,1)S(1)} %convert_bitcast_fusion), channel_id=1, replica_groups=mesh['dp'=4,'expert'=8] {'dp','expert'}, dimensions={0}, use_global_device_ids=true | all-gather | bytes 4224 | tf_op jit(solution)/shard_map/all_gather | solution.py:67
  43.4 37.1 %all-gather.7.cloned.1.call-done = bf16[1024,3072]{1,0:T(8,128)(2,1)} async-done(((bf16[32,3072]{1,0:T(8,128)(2,1)}), bf16[1024,3072]{1,0:T(8,128)(2,1)}) %all-gather.7.cloned.1.call-update) | async-done | bytes 6291472 | tf_op jit(solution)/shard_map/all_gather | solution.py:66
  85.1 4.5 reduce-window.6
  91.0 4.3 scatter_custom_fusion.1
  95.4 4.3 scatter_custom_fusion
  100.0 4.3 scatter_custom_fusion.2
  104.5 5.1 gather_fusion.2
  109.6 3.7 select_convert_fusion
  113.2 6.6 all-to-all-start.2
  121.2 59.0 %all-gather = bf16[1,1024]{1,0:T(2,128)(2,1)S(1)} all-gather(bf16[1,128]{1,0:T(2,128)(2,1)S(1)} %convert_element_type.145), channel_id=2, replica_groups=mesh['dp'=4,'expert'=8] {'expert'}, dimensions={1}, use_global_device_ids=true | all-gather | bytes 2304 | tf_op jit(solution)/shard_map/all_gather | solution.py:138
  183.2 4.5 while.50
  190.1 7.9 while.51
  203.0 5.0 gather_fusion
  208.0 3.3 broadcast_select_fusion
  211.3 5.4 all-to-all-start
  216.7 3.3 copy.119
  220.0 48.8 %all-to-all-done = bf16[16,72,1024]{2,1,0:T(8,128)(2,1)S(1)} async-done(((bf16[16,72,1024]{2,1,0:T(8,128)(2,1)}), bf16[16,72,1024]{2,1,0:T(8,128)(2,1)S(1)}, u32[]{:S(2)}, u32[]{:S(2)}) %all-to-all-start) | async-done | bytes 2359328 | tf_op jit(solution)/shard_map/all_to_all | solution.py:76
  270.5 5.2 fusion.40
  275.9 3.6 multiply_convert_fusion.1
  281.0 3.8 copy.116
  284.8 6.3 all-to-all-start.1
  291.1 5.6 fusion.49
  296.7 3.8 copy.120
  300.5 42.7 %all-to-all-done.1 = bf16[2,576,1024]{2,0,1:T(2,128)(2,1)S(1)} async-done(((bf16[2,576,1024]{2,0,1:T(2,128)(2,1)}), bf16[2,576,1024]{2,0,1:T(2,128)(2,1)S(1)}, u32[]{:S(2)}, u32[]{:S(2)}) %all-to-all-start.1) | async-done | bytes 2359328 | tf_op jit(solution)/shard_map/all_to_all | solution.py:80
  343.2 6.9 all-to-all-start.3
  352.6 49.7 %all-to-all-done.3 = bf16[2,576,1024]{2,0,1:T(2,128)(2,1)} async-done(((bf16[2,576,1024]{2,0,1:T(2,128)(2,1)}), bf16[2,576,1024]{2,0,1:T(2,128)(2,1)}, u32[]{:S(2)}, u32[]{:S(2)}) %all-to-all-start.3) | async-done | bytes 2359328 | tf_op jit(solution)/shard_map/all_to_all | solution.py:80
  402.3 3.8 copy.121
  406.0 5.4 gather_fusion.1
  411.4 8.2 gather_fusion.3
  419.6 5.0 convert_reduce_fusion
  428.2 5.4 while.52
  437.7 22.0 %while.53 = (s32[]{:T(128)}, f32[128,8,2,64]{0,3,2,1:T(8,128)}, f32[1024,512]{0,1:T(8,128)}, f32[1024,512]{0,1:T(8,128)}, s32[]{:T(128)}, /*index=5*/bf16[1024,5...) while((s32[]{:T(128)}, f32[128,8,2,64]{0,3,2,1:T(8,128)}, ...), condition=%wide.region_21.22_spmd.clone, body=%wide.region_20.21_spmd.clone.sunk | while | flops 682295936 | bytes 64720732 | solution.py:314
  461.4 4.6 convolution_convert_fusion.2
  465.9 5.1 convolution_convert_fusion
  473.4 18.9 %reduce-scatter.8.cloned.1.call-done = f32[128,512]{0,1:T(8,128)} async-done(((f32[1024,512]{0,1:T(8,128)}), f32[128,512]{0,1:T(8,128)}) %reduce-scatter.8.cloned.1.call-update) | async-done | bytes 262160 | tf_op jit(solution)/shard_map/reduce_scatter | solution.py:316
  495.0 34.1 %reduce-scatter.10.cloned.1.call-done = f32[128,512]{0,1:T(8,128)} async-done(((f32[1024,512]{0,1:T(8,128)}), f32[128,512]{0,1:T(8,128)}) %reduce-scatter.10.cloned.1.call-update) | async-done | bytes 262160 | tf_op jit(solution)/shard_map/reduce_scatter | solution.py:317
  530.1 4.7 fusion.68
  536.2 5.5 pad_maximum_fusion.1
  544.8 4.8 pad_maximum_fusion
  552.8 3.6 copy.128
  556.4 3.5 copy.129
  559.9 96.6 %reduce-scatter.16.cloned.1.call-done = f32[32,2]{1,0:T(8,128)} async-done(((f32[1024,2]{1,0:T(8,128)}), f32[32,2]{1,0:T(8,128)}) %reduce-scatter.16.cloned.1.call-update) | async-done | bytes 272
  658.0 84.4 %reduce-scatter.14.cloned.1.call-done = bf16[2,256,1536]{1,2,0:T(8,128)(2,1)} async-done(((bf16[2,1024,1536]{1,2,0:T(8,128)(2,1)}), bf16[2,256,1536]{1,2,0:T(8,128)(2,1)}) %reduce-scatter.14.cloned.1.call-update) | async-done | bytes 1572880 | tf_op jit(solution)/shard_map/reduce_scatter | solution.py:341
  745.2 158.9 %reduce-scatter.12.cloned.1.call-done = f32[32,3072]{1,0:T(8,128)} async-done(((f32[1024,3072]{1,0:T(8,128)}), f32[32,3072]{1,0:T(8,128)}) %reduce-scatter.12.cloned.1.call-update) | async-done | bytes 393232 | tf_op jit(solution)/shard_map/reduce_scatter | solution.py:338
  910.0 39.2 %psum.7 = f32[]{:T(128)} all-reduce(f32[]{:T(128)S(6)} %add.282), channel_id=1, replica_groups=mesh['dp'=4,'expert'=8] {'dp','expert'}, use_global_device_ids=true, to_apply=%region_33.34 | all-reduce | flops 1 | bytes 8 | tf_op jit(solution)/shard_map/psum | solution.py:352
  949.9 6.6 multiply_subtract_fusion
  956.5 3.5 copy.132
  960.0 3.7 copy.133
  (296 shorter events, 101.8 us)
Async XLA Ops:
  7.2 73.4 %all-gather.7.cloned.1.call-start = ((), (), s32[]{:S(2)}) async-start(), calls=%async_computation.9 | async-start | bytes 6488064 | tf_op jit(solution)/shard_map/all_gather | solution.py:66
  8.9 172.8 %all-gather.11.cloned.1.call-start = ((), (), s32[]{:S(2)}) async-start(), calls=%async_computation.11 | async-start | bytes 1179648 | tf_op jit(solution)/shard_map/all_gather | solution.py:136
  42.1 139.5 %copy-start.26 = (f32[128,64]{0,1:T(8,128)}, f32[128,64]{0,1:T(8,128)S(1)}, u32[]{:S(2)}) copy-start(f32[128,64]{0,1:T(8,128)S(1)} %get-tuple-element.649) | copy-start | bytes 98308
  42.1 139.5 %copy-start.28 = (f32[128,64]{0,1:T(8,128)}, f32[128,64]{0,1:T(8,128)S(1)}, u32[]{:S(2)}) copy-start(f32[128,64]{0,1:T(8,128)S(1)} %get-tuple-element.648) | copy-start | bytes 98308
  43.4 37.2 %copy-start.41 = (f32[128]{0:T(128)}, f32[128]{0:T(128)S(1)}, u32[]{:S(2)}) copy-start(f32[128]{0:T(128)S(1)} %fusion.72) | copy-start | bytes 1540
  43.4 37.2 %copy-start.36 = (f32[128]{0:T(128)}, f32[128]{0:T(128)S(1)}, u32[]{:S(2)}) copy-start(f32[128]{0:T(128)S(1)} %fusion.101) | copy-start | bytes 1540
  43.4 37.1 %copy-start.32 = (f32[1024,1]{0,1:T(1,128)}, f32[1024,1]{0,1:T(1,128)S(1)}, u32[]{:S(2)}) copy-start(f32[1024,1]{0,1:T(1,128)S(1)} %get-tuple-element.651) | copy-start | bytes 12292
  83.6 20.8 %copy-start.21 = (f32[128,2048]{1,0:T(8,128)}, f32[128,2048]{1,0:T(8,128)S(1)}, u32[]{:S(2)}) copy-start(f32[128,2048]{1,0:T(8,128)S(1)} %fusion.44) | copy-start | bytes 3145732
  83.6 16.1 %copy-start.34 = (f32[1,128,8]{1,2,0:T(8,128)S(1)}, f32[1,128,8]{1,2,0:T(8,128)}, u32[]{:S(2)}) copy-start(f32[1,128,8]{1,2,0:T(8,128)} %param.26) | copy-start | bytes 12292
  83.7 20.8 %copy-start.22 = (bf16[1,128,1024]{2,1,0:T(8,128)(2,1)S(1)}, bf16[1,128,1024]{2,1,0:T(8,128)(2,1)}, u32[]{:S(2)}) copy-start(bf16[1,128,1024]{2,1,0:T(8,128)(2,1)} %param.27) | copy-start | bytes 786436
  84.8 103.0 %all-gather.9.cloned.1.call-start = ((), (), s32[]{:S(2)}) async-start(), calls=%async_computation.10 | async-start | bytes 1179648 | tf_op jit(solution)/shard_map/all_gather | solution.py:137
  113.2 6.6 copy-start.5
  113.2 98.1 %all-to-all-start.2 = ((bf16[16,72,1024]{2,1,0:T(8,128)(2,1)}), bf16[16,72,1024]{2,1,0:T(8,128)(2,1)}, u32[]{:S(2)}, u32[]{:S(2)}) async-start(bf16[16,72,1024]{2,1,0:T(8,128)(2,1)} %select_convert_fusion), calls=%async_computation.2 | async-start | bytes 4718592 | tf_op jit(solution)/shard_map/all_to_all | solution.py:76
  119.8 150.6 %all-gather.13.cloned.1.call-start = ((), (), s32[]{:S(2)}) async-start(), calls=%async_computation.12 | async-start | bytes 7864320 | tf_op jit(solution)/shard_map/all_gather | solution.py:72
  198.0 4.1 copy-start
  198.0 10.0 %copy-start.2 = (bf16[1024,512]{0,1:T(8,128)(2,1)}, bf16[1024,512]{0,1:T(8,128)(2,1)S(1)}, u32[]{:S(2)}) copy-start(bf16[1024,512]{0,1:T(8,128)(2,1)S(1)} %get-tuple-element.1140) | copy-start | bytes 3145732
  199.5 2.7 copy-start.24
  211.3 57.5 %all-to-all-start = ((bf16[16,72,1024]{2,1,0:T(8,128)(2,1)}), bf16[16,72,1024]{2,1,0:T(8,128)(2,1)S(1)}, u32[]{:S(2)}, u32[]{:S(2)}) async-start(bf16[16,72,1024]{2,1,0:T(8,128)(2,1)} %broadcast_select_fusion), calls=%async_computation | async-start | bytes 4718592 | tf_op jit(solution)/shard_map/all_to_all | solution.py:76
  270.5 5.3 copy-start.16
  270.5 5.5 copy-start.43
  284.8 58.4 %all-to-all-start.1 = ((bf16[2,576,1024]{2,0,1:T(2,128)(2,1)}), bf16[2,576,1024]{2,0,1:T(2,128)(2,1)S(1)}, u32[]{:S(2)}, u32[]{:S(2)}) async-start(bf16[2,576,1024]{2,0,1:T(2,128)(2,1)} %copy.116), calls=%async_computation.1 | async-start | bytes 4718592 | tf_op jit(solution)/shard_map/all_to_all | solution.py:80
  343.2 7.0 copy-start.6
  343.2 59.1 %all-to-all-start.3 = ((bf16[2,576,1024]{2,0,1:T(2,128)(2,1)}), bf16[2,576,1024]{2,0,1:T(2,128)(2,1)}, u32[]{:S(2)}, u32[]{:S(2)}) async-start(bf16[2,576,1024]{2,0,1:T(2,128)(2,1)} %copy.120), calls=%async_computation.3 | async-start | bytes 4718592 | tf_op jit(solution)/shard_map/all_to_all | solution.py:80
  350.1 142.3 %reduce-scatter.8.cloned.1.call-start = ((), (), s32[]{:S(2)}) async-start(), calls=%async_computation.13 | async-start | bytes 2359296 | tf_op jit(solution)/shard_map/reduce_scatter | solution.py:316
  411.4 8.2 copy-start.11
  419.6 5.0 copy-start.14
  419.6 5.2 copy-start.23
  424.8 3.4 copy-start.1
  424.8 3.4 copy-start.3
  425.7 116.1 %copy-start.12 = (f32[128,1024]{1,0:T(8,128)}, f32[128,1024]{1,0:T(8,128)S(1)}, u32[]{:S(2)}) copy-start(f32[128,1024]{1,0:T(8,128)S(1)} %get-tuple-element.640) | copy-start | bytes 1572868
  459.7 69.4 %reduce-scatter.10.cloned.1.call-start = ((), (), s32[]{:S(2)}) async-start(), calls=%async_computation.14 | async-start | bytes 2359296 | tf_op jit(solution)/shard_map/reduce_scatter | solution.py:317
  460.3 196.3 %reduce-scatter.16.cloned.1.call-start = ((), (), s32[]{:S(2)}) async-start(), calls=%async_computation.17 | async-start | bytes 540672
  461.3 4.6 copy-start.18
  461.3 4.6 copy-start.45
  461.3 4.6 copy-start.46
  465.9 5.1 copy-start.27
  472.1 57.9 %copy-start.15 = (bf16[1,128,1024]{2,1,0:T(8,128)(2,1)S(1)}, bf16[1,128,1024]{2,1,0:T(8,128)(2,1)}, u32[]{:S(2)}) copy-start(bf16[1,128,1024]{2,1,0:T(8,128)(2,1)} %param.23) | copy-start | bytes 786436
  472.2 57.9 %copy-start.33 = (f32[1024,1]{0,1:T(1,128)S(1)}, f32[1024,1]{0,1:T(1,128)}, u32[]{:S(2)}) copy-start(f32[1024,1]{0,1:T(1,128)} %copy-done.32) | copy-start | bytes 12292
  472.2 57.9 %copy-start.37 = (f32[128]{0:T(128)S(1)}, f32[128]{0:T(128)}, u32[]{:S(2)}) copy-start(f32[128]{0:T(128)} %copy-done.36) | copy-start | bytes 1540
  530.1 6.1 copy-start.19
  535.9 206.5 %reduce-scatter.14.cloned.1.call-start = ((), (), s32[]{:S(2)}) async-start(), calls=%async_computation.16 | async-start | bytes 7864320 | tf_op jit(solution)/shard_map/reduce_scatter | solution.py:341
  541.8 362.4 %reduce-scatter.12.cloned.1.call-start = ((), (), s32[]{:S(2)}) async-start(), calls=%async_computation.15 | async-start | bytes 12976128 | tf_op jit(solution)/shard_map/reduce_scatter | solution.py:338
  556.4 3.6 copy-start.42
  960.0 3.7 copy-start.4
  963.7 2.4 copy-start.38
  963.7 2.4 copy-start.39
  963.7 2.4 copy-start.40
  963.7 3.0 copy-start.20
  (16 other events, 23.3 us)
Sparse Core Ops, SparseCore 0:
  11.6 68.9 all-gather.6
  84.9 20.7 all-gather.10
  107.8 32.6 all-gather.8
  142.8 70.7 all-gather.12
  459.8 32.4 reduce-scatter.7
  494.5 34.5 reduce-scatter.9
  536.0 120.4 reduce-scatter.15
  659.8 82.5 reduce-scatter.13
  749.5 154.6 reduce-scatter.11
where the time goes:
time: 989 us; the launch traced here: 977 us
  waiting for transfers between devices  572 us (58%)
  blocking collectives  130 us (13%)
  local copies, waits for them, and re-layouts  101 us (10%)
  matrix products  65.7 us (7%)
  other arithmetic  62.1 us (6%)
  starting transfers between devices  25.7 us (3%)
  between operations  19.7 us (2%)
    reduce_scatter x1, waiting for transfers between devices, body(): lax.psum_scatter(attn_partial, ('dp', 'expert'), scatter_dimension=0, til...  159 us
    unnamed x10, waiting for transfers between devices  97.3 us
    all_to_all x2, waiting for transfers between devices, to_sender(): lax.all_to_all(buffer, 'expert', split_axis=1, concat_axis=0, tiled=True)  92.4 us
    reduce_scatter x1, waiting for transfers between devices, body(): lax.psum_scatter(jnp.concatenate([inward_grad, down_grad], axis=2).astype...  84.4 us
    all_gather x1, blocking collectives, body(): lax.all_gather(doc_ids[0].astype(jnp.bfloat16), 'expert', axis=0, tiled=T...  59 us
    all_to_all x2, waiting for transfers between devices, to_owner(): lax.all_to_all(buffer, 'expert', split_axis=0, concat_axis=1, tiled=True)  48.8 us
    psum x1, blocking collectives, body(): grad_norm = jnp.sqrt(lax.psum(local_squares, ('dp', 'expert')))  39.2 us
    all_gather x1, waiting for transfers between devices, attn_fetch(): lax.all_gather(w_attn.astype(jnp.bfloat16), ('dp', 'expert'), axis=0, til...  37.1 us
  transfers between devices with their start and end apart: 13, of which 9 were waited for; matrix products, arithmetic and copies ran while one was open for 12% of the time, Pallas kernels for 0%

commit v1 on v0

--- a/solution.py
+++ b/solution.py
@@ -2,6 +2,9 @@
 import jax.numpy as jnp
 from jax import lax
 from jax.sharding import PartitionSpec as P
+import numpy as np
+from jax.experimental import pallas as pl
+from jax.experimental.pallas import tpu as pltpu
 
 D = 1024
 H = 16
@@ -88,7 +91,7 @@
     return (gate_up, activated)
 
 
-def body(
+def general_body(
     activations,
     doc_ids,
     routes,
@@ -389,6 +392,552 @@
     )
 
 
+def fits(mesh):
+    return dict(mesh.shape) == {"dp": 4, "expert": KVH}
+
+
+def half_turn(tile):
+    lane = lax.broadcasted_iota(jnp.int32, tile.shape, tile.ndim - 1)
+    ahead = jnp.roll(tile, -(HD // 2), axis=-1)
+    behind = jnp.roll(tile, HD // 2, axis=-1)
+    return jnp.where(lane % HD < HD // 2, ahead, behind)
+
+
+def head_tables(length):
+    cosine, sine = rope_tables(jnp.arange(length, dtype=jnp.int32), HD)
+    cosine, sine = cosine[:, 0], sine[:, 0]
+    lane = jnp.arange(HD)
+    signed = jnp.where(lane < HD // 2, -sine, sine)
+    ones, zeros = jnp.ones_like(cosine), jnp.zeros_like(sine)
+    return (
+        jnp.concatenate([cosine, cosine, cosine, ones], axis=1),
+        jnp.concatenate([signed, signed, signed, zeros], axis=1),
+    )
+
+
+def group_columns(weights, groups):
+    rows = weights.shape[0]
+    parts = [
+        weights[:, :QD].reshape(rows, groups, -1),
+        weights[:, QD : QD + KVD].reshape(rows, groups, -1),
+        weights[:, QD + KVD : QKV].reshape(rows, groups, -1),
+        weights[:, QKV:].reshape(rows, groups, -1),
+    ]
+    return jnp.concatenate(parts, axis=2).transpose(1, 0, 2)
+
+
+def ungroup_columns(grouped):
+    rows = grouped.shape[1]
+    g = grouped.transpose(1, 0, 2)
+    parts = [g[:, :, :128], g[:, :, 128:192], g[:, :, 192:256], g[:, :, 256:]]
+    return jnp.concatenate([p.reshape(rows, -1) for p in parts], axis=1)
+
+
+def remote(source, target, sent, landed, device):
+    return pltpu.make_async_remote_copy(
+        src_ref=source,
+        dst_ref=target,
+        send_sem=sent,
+        recv_sem=landed,
+        device_id=device,
+        device_id_type=pl.DeviceIdType.MESH,
+    )
+
+
+def whereabouts():
+    i, e = lax.axis_index("dp"), lax.axis_index("expert")
+    return i, e, e // 2, lax.rem(e, 2)
+
+
+def greet(i, e):
+    barrier = pltpu.get_barrier_semaphore()
+    others = [(i, lax.rem(e + k, SPAN)) for k in range(1, SPAN)]
+    others += [(lax.rem(i + k, PLANE), e) for k in range(1, PLANE)]
+    for device in others:
+        pl.semaphore_signal(barrier, inc=1, device_id=device, device_id_type=pl.DeviceIdType.MESH)
+    pl.semaphore_wait(barrier, len(others))
+
+
+class LineGather:
+    def __init__(self, slot, where, sent, passed, landed):
+        self.slot, self.where = slot, where
+        self.sent, self.passed, self.landed = sent, passed, landed
+        self.live = []
+
+    def _copy(self, source, index, sem, device):
+        place = self.slot(index)
+        return remote(place if source is None else source, place, sem, self.landed.at[index], device)
+
+    def start(self, source=None):
+        i, e, z, c = self.where
+        for k in range(1, LINE):
+            there = lax.rem(z + k, LINE) * 2 + c
+            copy = self._copy(source, e, self.sent.at[k], (i, there))
+            copy.start()
+            self.live.append(copy)
+        copy = self._copy(source, e, self.sent.at[0], (i, z * 2 + 1 - c))
+        copy.start()
+        self.live.append(copy)
+
+    def wait(self, index):
+        i, e, z, c = self.where
+        self._copy(None, index, self.sent.at[0], (i, z * 2 + 1 - c)).wait_recv()
+
+    def sibling(self):
+        _, e, z, c = self.where
+        return z * 2 + 1 - c
+
+    def near(self, k):
+        _, e, z, c = self.where
+        return lax.rem(z + k, LINE) * 2 + c
+
+    def far(self, k):
+        _, e, z, c = self.where
+        return lax.rem(z + k, LINE) * 2 + 1 - c
+
+    def forward(self, k):
+        i, e, z, c = self.where
+        index = self.near(k)
+        self.wait(index)
+        copy = self._copy(None, index, self.passed.at[k - 1], (i, z * 2 + 1 - c))
+        copy.start()
+        self.live.append(copy)
+
+    def rest(self):
+        self.wait(self.sibling())
+        for k in range(1, LINE):
+            self.wait(self.far(k))
+
+    def drain(self):
+        for copy in self.live:
+            copy.wait_send()
+
+
+def half_turn_tile(tile):
+    pieces = []
+    for first in range(0, tile.shape[1], 128):
+        part = tile[:, first : first + 128]
+        lane = lax.broadcasted_iota(jnp.int32, part.shape, 1)
+        ahead = pltpu.roll(part, 128 - HD // 2, 1)
+        behind = pltpu.roll(part, HD // 2, 1)
+        pieces.append(jnp.where(lax.rem(lane, HD) < HD // 2, ahead, behind))
+    return jnp.concatenate(pieces, axis=1)
+
+
+def rms_rows(values):
+    return lax.rsqrt(jnp.mean(values * values, axis=-1, keepdims=True) + EPSILON)
+
+
+def dot(a, b, contract):
+    return lax.dot_general(a, b, (contract, ((), ())), preferred_element_type=jnp.float32)
+
+
+NN, NT, TN = ((1,), (0,)), ((1,), (1,)), ((0,), (0,))
+LINE, SPAN, PLANE = 4, 8, 4
+QUERY_BLOCK = 256
+
+
+def block_view(first, reach):
+    return max(0, first - reach), first + QUERY_BLOCK
+
+
+def visible_keys(first, low, high, docs_row, docs_col):
+    shape = (QUERY_BLOCK, high - low)
+    key = lax.broadcasted_iota(jnp.int32, shape, 1) + low
+    query = lax.broadcasted_iota(jnp.int32, shape, 0) + first
+    same = docs_row[:, low:high] == docs_col[first : first + QUERY_BLOCK]
+    return (key <= query) & same
+
+
+def start_kernel(
+    x_ref, up_ref, wq_ref, wo_ref, we_ref, pack_ref, cos_ref, sin_ref,
+    x_all, up_all, h1_all, qkv_ref, w_mine, wo_all, we_all, o_own, h2_ref, r_own, cols_ref, docs_ref, gains_ref,
+    o_all, r_all, pack_all, gain_sum,
+    x_sent, x_passed, x_landed, up_sent, up_passed, up_landed, o_sent, o_passed, o_landed,
+    wo_sent, wo_passed, wo_landed, wq_sent, wq_landed, pack_sent, pack_landed,
+    wqd_sent, wqd_landed, gd_sent, gd_landed, wod_sent, wod_landed, wod_passed, wod_far, we_sent, we_landed,
+):
+    f32, bf16 = jnp.float32, jnp.bfloat16
+    where = i, e, z, c = whereabouts()
+    sibling = (i, z * 2 + 1 - c)
+    rows = x_ref.shape[0]
+    length = rows * SPAN
+    local = we_ref.shape[0]
+    live = []
+
+    def go(*spec):
+        copy = remote(*spec)
+        copy.start()
+        live.append(copy)
+
+    greet(i, e)
+    for k in range(1, SPAN):
+        there = lax.rem(e + k, SPAN)
+        go(pack_ref.at[there], pack_all.at[e], pack_sent.at[k], pack_landed.at[e], (i, there))
+    for k in range(1, SPAN):
+        there = lax.rem(e + k, SPAN)
+        go(wq_ref.at[there], w_mine.at[i, e], wq_sent.at[k], wq_landed.at[e], (i, there))
+    x_gather = LineGather(lambda s: x_all.at[s], where, x_sent, x_passed, x_landed)
+    x_gather.start(x_ref)
+    for l in range(local):
+        for k in (1, 2, 3):
+            there = lax.rem(i + k, PLANE)
+            go(we_ref.at[l], we_all.at[l, i], we_sent.at[l, k], we_landed.at[l, i], (there, e))
+    pack_all[e] = pack_ref[e]
+    w_mine[i, e] = wq_ref[e]
+    x_all[e] = x_ref[...]
+    up_all[e] = up_ref[...]
+    wo_all[i, z, c] = wo_ref[...]
+    for l in range(local):
+        we_all[l, i] = we_ref[l]
+
+    for k in range(1, SPAN):
+        there = lax.rem(e + k, SPAN)
+        remote(pack_ref.at[there], pack_all.at[there], pack_sent.at[k], pack_landed.at[there], sibling).wait_recv()
+    for half in range(2):
+        summed = pack_all[4 * half]
+        for s in range(1, 4):
+            summed = summed + pack_all[4 * half + s]
+        gain_sum[i, half] = summed
+    for k in range(1, PLANE):
+        there = lax.rem(i + k, PLANE)
+        go(gain_sum.at[i], gain_sum.at[i], gd_sent.at[k], gd_landed.at[i], (there, e))
+    for k in range(1, SPAN):
+        there = lax.rem(e + k, SPAN)
+        remote(wq_ref.at[there], w_mine.at[i, there], wq_sent.at[k], wq_landed.at[there], sibling).wait_recv()
+    for k in range(1, PLANE):
+        there = lax.rem(i + k, PLANE)
+        go(w_mine.at[i], w_mine.at[i], wqd_sent.at[k], wqd_landed.at[i], (there, e))
+    for s in range(SPAN):
+        block = pack_all[s]
+        tall = jnp.concatenate([block, jnp.zeros((rows - block.shape[0], rows), f32)], axis=0)
+        cols_ref[s * rows : (s + 1) * rows] = tall.T
+        docs_ref[:, s * rows : (s + 1) * rows] = block
+    for k in range(1, PLANE):
+        there = lax.rem(i + k, PLANE)
+        remote(gain_sum.at[i], gain_sum.at[there], gd_sent.at[k], gd_landed.at[there], sibling).wait_recv()
+    for tile in range(2 * PLANE):
+        gains_ref[:, tile * 128 : (tile + 1) * 128] = gain_sum[tile // 2, tile % 2].astype(bf16).astype(f32)
+    gain_one = gains_ref[3:4]
+    gain_two = gains_ref[4:5]
+
+    def first_norm(s):
+        values = x_all[s].astype(f32)
+        h1_all[s] = (values * rms_rows(values) * gain_one).astype(bf16)
+
+    first_norm(e)
+    for k in range(1, LINE):
+        x_gather.forward(k)
+        first_norm(x_gather.near(k))
+    up_gather = LineGather(lambda s: up_all.at[s], where, up_sent, up_passed, up_landed)
+    wo_gather = LineGather(
+        lambda s: wo_all.at[i, s // 2, lax.rem(s, 2)], where, wo_sent, wo_passed, wo_landed
+    )
+    wo_gather.start(wo_ref)
+    up_gather.start(up_ref)
+    x_gather.wait(x_gather.sibling())
+    first_norm(x_gather.sibling())
+    for k in range(1, LINE):
+        x_gather.wait(x_gather.far(k))
+        first_norm(x_gather.far(k))
+    for k in range(1, PLANE):
+        there = lax.rem(i + k, PLANE)
+        remote(w_mine.at[i], w_mine.at[there], wqd_sent.at[k], wqd_landed.at[there], sibling).wait_recv()
+    weights = w_mine[...].reshape(PLANE * SPAN * w_mine.shape[2], 256)
+    for first in range(0, length, QUERY_BLOCK):
+        span = slice(first, first + QUERY_BLOCK)
+        slots = slice(first // rows, (first + QUERY_BLOCK) // rows)
+        raw = dot(h1_all[slots].reshape(QUERY_BLOCK, D), weights, NN)
+        qkv_ref[span] = (raw * cos_ref[span] + half_turn_tile(raw) * sin_ref[span]).astype(bf16)
+
+    own_cols = pl.ds(pl.multiple_of(e * 128, 128), 128)
+    docs_row = docs_ref[2:3]
+    docs_col = cols_ref[:, 2:3]
+    for first in range(0, length, QUERY_BLOCK):
+        low, high = block_view(first, length // 2)
+        visible = visible_keys(first, low, high, docs_row, docs_col)
+        span = slice(first, first + QUERY_BLOCK)
+        outs = []
+        for head in range(2):
+            q = qkv_ref[span, head * HD : (head + 1) * HD]
+            scores = dot(q, qkv_ref[low:high, 128:192], NT) * HD**-0.5
+            scores = jnp.where(visible, scores, -1e30)
+            raw = jnp.exp(scores - jnp.max(scores, axis=-1, keepdims=True))
+            probs = raw * (1.0 / jnp.sum(raw, axis=-1, keepdims=True))
+            outs.append(dot(probs.astype(bf16), qkv_ref[low:high, 192:256], NN))
+        both = jnp.concatenate(outs, axis=1).astype(bf16)
+        o_own[span] = both
+        o_all[span, own_cols] = both
+    o_gather = LineGather(
+        lambda s: o_all.at[:, pl.ds(pl.multiple_of(s * 128, 128), 128)], where, o_sent, o_passed, o_landed
+    )
+    o_gather.start(o_own)
+
+    for k in range(1, LINE):
+        wo_gather.forward(k)
+    for k in range(1, PLANE):
+        there = lax.rem(i + k, PLANE)
+        go(wo_all.at[i, :, c], wo_all.at[i, :, c], wod_sent.at[k], wod_landed.at[i], (there, e))
+    for k in range(1, LINE):
+        up_gather.forward(k)
+    wo_gather.rest()
+    for k in range(1, PLANE):
+        there = lax.rem(i + k, PLANE)
+        here = wo_all.at[there, :, c]
+        remote(here, here, wod_sent.at[k], wod_landed.at[there], sibling).wait_recv()
+        go(here, here, wod_passed.at[k], wod_far.at[there], sibling)
+    for k in range(1, LINE):
+        o_gather.forward(k)
+    for k in range(1, PLANE):
+        there = lax.rem(i + k, PLANE)
+        far = wo_all.at[there, :, 1 - c]
+        remote(far, far, wod_sent.at[k], wod_far.at[there], sibling).wait_recv()
+    o_gather.rest()
+    w_out = wo_all[...].reshape(D, D)
+    for first in range(0, length, QUERY_BLOCK):
+        span = slice(first, first + QUERY_BLOCK)
+        slots = slice(first // rows, (first + QUERY_BLOCK) // rows)
+        values = x_all[slots].reshape(QUERY_BLOCK, D).astype(f32) + dot(o_all[span], w_out, NT)
+        r_all[slots] = values.reshape(-1, rows, D)
+        h2_ref[span] = (values * rms_rows(values) * gain_two).astype(bf16)
+    r_own[...] = r_all[e]
+    up_gather.rest()
+    for l in range(local):
+        for k in (1, 2, 3):
+            there = lax.rem(i + k, PLANE)
+            remote(we_ref.at[l], we_all.at[l, there], we_sent.at[l, k], we_landed.at[l, there], sibling).wait_recv()
+    for copy in live:
+        copy.wait_send()
+    for gather in (x_gather, up_gather, wo_gather, o_gather):
+        gather.drain()
+
+
+def call_start(x, up, wq, wo, we, pack, cosine, sine):
+    f32, bf16 = jnp.float32, jnp.bfloat16
+    rows, local = x.shape[0], we.shape[0]
+    length = rows * SPAN
+    part = wo.shape[0]
+    shaped = jax.ShapeDtypeStruct
+    vmem = pl.BlockSpec(memory_space=pltpu.VMEM)
+    outs = [
+        shaped((SPAN, rows, D), bf16),
+        shaped((SPAN, rows, D), bf16),
+        shaped((SPAN, rows, D), bf16),
+        shaped((length, 256), bf16),
+        shaped((PLANE, SPAN, part, 256), bf16),
+        shaped((PLANE, LINE, 2, part, D), bf16),
+        shaped((local, PLANE, we.shape[1], 3 * FF), bf16),
+        shaped((length, 128), bf16),
+        shaped((length, D), bf16),
+        shaped((rows, D), f32),
+        shaped((length, 128), f32),
+        shaped((8, length), f32),
+        shaped((8, D), f32),
+    ]
+    dma = pltpu.SemaphoreType.DMA
+    line = [dma((LINE,)), dma((LINE - 1,)), dma((SPAN,))]
+    scratch = [
+        pltpu.VMEM((length, D), bf16),
+        pltpu.VMEM((SPAN, rows, D), f32),
+        pltpu.VMEM((SPAN, 8, rows), f32),
+        pltpu.VMEM((PLANE, 2, 8, 128), f32),
+        *line, *line, *line, *line,
+        dma((SPAN,)), dma((SPAN,)), dma((SPAN,)), dma((SPAN,)),
+        dma((PLANE,)), dma((PLANE,)), dma((PLANE,)), dma((PLANE,)),
+        dma((PLANE,)), dma((PLANE,)), dma((PLANE,)), dma((PLANE,)),
+        dma((local, PLANE)), dma((local, PLANE)),
+    ]
+    return pl.pallas_call(
+        start_kernel,
+        out_shape=outs,
+        in_specs=[vmem] * 8,
+        out_specs=[vmem] * len(outs),
+        scratch_shapes=scratch,
+        compiler_params=pltpu.CompilerParams(
+            collective_id=0, has_side_effects=True, vmem_limit_bytes=60 * 2**20
+        ),
+        name="start",
+    )(x, up, wq, wo, we, pack, cosine, sine)
+
+
+def expert_kernel(h2_ref, up_ref, we_ref, cols_ref, y_ref, d_ref, act_ref, dgu_ref, y_sum, d_sum):
+    f32, bf16 = jnp.float32, jnp.bfloat16
+    local = we_ref.shape[0]
+    size = 256
+    for l in range(local):
+        weights = we_ref[l].reshape(D, 3 * FF)
+
+        def step(b, _, l=l, weights=weights):
+            span = pl.ds(pl.multiple_of(b * size, size), size)
+            gate = cols_ref[span, l : l + 1]
+            routed = gate > 0
+            gu = dot(h2_ref[span], weights[:, : 2 * FF], NN)
+            g, u = gu[:, :FF], gu[:, FF:]
+            sig = 1.0 / (1.0 + jnp.exp(-g))
+            act = jnp.where(routed, g * sig * u, 0.0).astype(bf16)
+            act_ref[l, span] = act
+            y = gate * dot(act, weights[:, 2 * FF :], NT).astype(bf16).astype(f32)
+            dy = (gate * up_ref[span].astype(f32)).astype(bf16)
+            dact = dot(dy, weights[:, 2 * FF :], NN)
+            dg = dact * u * sig * (1.0 + g * (1.0 - sig))
+            du = dact * g * sig
+            dgu = jnp.where(routed, jnp.concatenate([dg, du], axis=1), 0.0).astype(bf16)
+            dgu_ref[l, span] = dgu
+            d = dot(dgu, weights[:, : 2 * FF], NT).astype(bf16).astype(f32)
+            if l == 0:
+                y_sum[span] = y
+                d_sum[span] = d
+            elif l < local - 1:
+                y_sum[span] += y
+                d_sum[span] += d
+            else:
+                y_ref[span] = (y_sum[span] + y).astype(bf16)
+                d_ref[span] = (d_sum[span] + d).astype(bf16)
+            return 0
+
+        lax.fori_loop(0, h2_ref.shape[0] // size, step, 0)
+
+
+def call_experts(h2, up, we, cols):
+    f32, bf16 = jnp.float32, jnp.bfloat16
+    length, local = h2.shape[0], we.shape[0]
+    shaped = jax.ShapeDtypeStruct
+    vmem = pl.BlockSpec(memory_space=pltpu.VMEM)
+    outs = [
+        shaped((length, D), bf16),
+        shaped((length, D), bf16),
+        shaped((local, length, FF), bf16),
+        shaped((local, length, 2 * FF), bf16),
+    ]
+    return pl.pallas_call(
+        expert_kernel,
+        out_shape=outs,
+        in_specs=[vmem] * 4,
+        out_specs=[vmem] * 4,
+        scratch_shapes=[pltpu.VMEM((length, D), f32)] * 2,
+        compiler_params=pltpu.CompilerParams(vmem_limit_bytes=60 * 2**20),
+        name="experts",
+    )(h2, up, we, cols)
+
+
+def fast_body(
+    activations,
+    doc_ids,
+    routes,
+    gate_weights,
+    cotangent,
+    step_count,
+    w_attn,
+    norm_gains,
+    w_expert,
+    first_attn,
+    second_attn,
+    first_gains,
+    second_gains,
+    first_expert,
+    second_expert,
+):
+    f32, bf16 = jnp.float32, jnp.bfloat16
+    rows = activations.shape[1]
+    span = lax.axis_size("expert")
+    place = lax.axis_index("expert")
+    length = rows * span
+    local = w_expert.shape[0]
+    total = local * span
+    own = lambda v, size: lax.dynamic_slice_in_dim(v, place * size, size, 0)
+    wa = w_attn.astype(bf16)
+    grouped = group_columns(wa, span)[:, :, :256]
+    hits = routes[0][:, :, None] == jnp.arange(total, dtype=jnp.int32)
+    dense = jnp.sum(jnp.where(hits, gate_weights[0][:, :, None], 0.0), axis=1).T
+    low = norm_gains.T
+    lane = jnp.arange(rows)
+    index = lax.axis_index("dp") * span + place
+    spread = jnp.where(lane // low.shape[1] == index % (rows // low.shape[1]), jnp.tile(low, (1, rows // low.shape[1])), 0.0)
+    shared = jnp.concatenate([doc_ids.astype(f32), spread], axis=0)
+    pack = jnp.concatenate(
+        [
+            dense.reshape(span, local, rows),
+            jnp.broadcast_to(shared[None], (span, 3, rows)),
+            jnp.zeros((span, 8 - local - 3, rows), f32),
+        ],
+        axis=1,
+    )
+    cosine, sine = head_tables(length)
+    x_all, up_all, h1, qkv, w_mine, w_out, w_exp, o, h2, r_own, cols, docs, gains = call_start(
+        activations[0], cotangent[0], grouped, wa[:, QKV:], w_expert.astype(bf16), pack, cosine, sine
+    )
+    x_all, up_all, h1 = (v.reshape(length, D) for v in (x_all, up_all, h1))
+    w_mine, w_out = w_mine.reshape(D, 256), w_out.reshape(D, D)
+    gain_one, gain_two = gains[3], gains[4]
+    y_part, d_part, act, dgu = call_experts(h2, up_all, w_exp, cols)
+    grads = []
+    for e in range(local):
+        dy = (cols[:, e : e + 1] * up_all.astype(f32)).astype(bf16)
+        inward = jnp.einsum("td,tf->df", h2, dgu[e], preferred_element_type=f32)
+        down = jnp.einsum("td,tf->df", dy, act[e], preferred_element_type=f32)
+        grads.append(jnp.concatenate([inward, down], axis=1))
+    ge = jnp.stack(grads).astype(bf16)
+    q = qkv[:, :128].reshape(length, 2, HD)
+    k, v = qkv[:, 128:192], qkv[:, 192:]
+    pos = jnp.arange(length)
+    visible = (pos[None, :] <= pos[:, None]) & (docs[2][None, :] == cols[:, 2:3])
+    s = jnp.einsum("thd,ud->htu", q, k, preferred_element_type=f32) * HD**-0.5
+    s = jnp.where(visible, s, -1e30)
+    peak = jnp.max(s, axis=-1, keepdims=True)
+    raw = jnp.exp(s - peak)
+    probs = raw / jnp.sum(raw, axis=-1, keepdims=True)
+    p16 = probs.astype(bf16)
+    combined = lax.psum_scatter(y_part.astype(bf16), "expert", scatter_dimension=0, tiled=True)
+    dh2 = lax.psum_scatter(d_part.astype(bf16), "expert", scatter_dimension=0, tiled=True).astype(f32)
+    x_own = activations[0].astype(f32)
+    block = (r_own + combined.astype(f32)).astype(bf16)
+    _, pull = jax.vjp(rms_scale, r_own, gain_two)
+    dr, gn2 = pull(dh2)
+    dr = cotangent[0].astype(f32) + dr
+    da = lax.all_gather(dr.astype(bf16), "expert", axis=0, tiled=True)
+    wo_mine = lax.dynamic_slice_in_dim(w_out, place * 128, 128, 1)
+    do = jnp.dot(da, wo_mine, preferred_element_type=f32).astype(bf16)
+    gwo = jnp.einsum("td,tc->dc", da, o, preferred_element_type=f32)
+    do2 = do.reshape(length, 2, HD)
+    dp = jnp.einsum("thd,ud->htu", do2, v, preferred_element_type=f32)
+    delta = jnp.sum(probs * dp, axis=-1, keepdims=True)
+    ds = (probs * (dp - delta)).astype(bf16)
+    dq = jnp.einsum("htu,ud->thd", ds, k, preferred_element_type=f32) * HD**-0.5
+    dk = jnp.einsum("htu,thd->ud", ds, q, preferred_element_type=f32) * HD**-0.5
+    dv = jnp.einsum("htu,thd->ud", p16, do2, preferred_element_type=f32)
+    dqkv = jnp.concatenate([dq.reshape(length, 128), dk, dv], axis=1)
+    dqkv = (dqkv * cosine - half_turn(dqkv) * sine).astype(bf16)
+    gqkv = jnp.einsum("td,tc->dc", h1, dqkv, preferred_element_type=f32)
+    dh1_part = jnp.einsum("tc,dc->td", dqkv, w_mine, preferred_element_type=f32)
+    dh1 = lax.psum_scatter(dh1_part.astype(bf16), "expert", scatter_dimension=0, tiled=True).astype(f32)
+    _, pull = jax.vjp(rms_scale, x_own, gain_one)
+    dx, gn1 = pull(dh1)
+    input_total = dr + dx
+    ga = jnp.concatenate([gqkv, gwo], axis=1).astype(bf16)
+    ga = lax.psum_scatter(ga, "dp", scatter_dimension=0, tiled=True)
+    squares = jnp.sum(ga.astype(f32) ** 2)
+    ga = lax.all_to_all(ga.reshape(span, -1, 384), "expert", 0, 0, tiled=True)
+    grad_attn = ungroup_columns(ga).astype(f32)
+    grad_expert = lax.psum_scatter(ge, "dp", scatter_dimension=1, tiled=True).astype(f32)
+    grad_gains = lax.psum_scatter(
+        jnp.stack([gn1, gn2], axis=1), ("dp", "expert"), scatter_dimension=0, tiled=True
+    )
+    squares = squares + jnp.sum(grad_gains**2) + jnp.sum(grad_expert**2)
+    grad_norm = jnp.sqrt(lax.psum(squares, ("dp", "expert")))
+    clip = jnp.minimum(1.0, CLIP_NORM / (grad_norm + 1e-06))
+    steps = step_count.astype(f32)
+    attn = adam_update(
+        w_attn, first_attn, second_attn, grad_attn * clip, steps, WEIGHT_DECAY, LEARN_RATE
+    )
+    gain = adam_update(
+        norm_gains, first_gains, second_gains, grad_gains * clip, steps, 0.0, GAIN_RATE
+    )
+    expert = adam_update(
+        w_expert, first_expert, second_expert, grad_expert * clip, steps, WEIGHT_DECAY, LEARN_RATE
+    )
+    return (block[None], input_total[None], grad_norm, *attn, *gain, *expert)
+
+
 def solution(mesh):
     in_specs = (
         P("dp", "expert", None),
@@ -421,4 +970,5 @@
         P("expert", "dp", None),
         P("expert", "dp", None),
     )
+    body = fast_body if fits(mesh) else general_body
     return jax.shard_map(body, mesh=mesh, in_specs=in_specs, out_specs=out_specs, check_vma=False)

time: 989 us -> 657 us (0.66)
  waiting for transfers between devices: 572 us -> 302 us
  Pallas kernels: 0 us -> 163 us
  blocking collectives: 130 us -> 40.6 us
  local copies, waits for them, and re-layouts: 101 us -> 37.8 us
  matrix products: 65.7 us -> 28.9 us
  starting transfers between devices: 25.7 us -> 5.82 us
  other arithmetic: 62.1 us -> 47.4 us
    pallas_call x0 -> x2, Pallas kernels: none -> 163 us  [the longest x1 138 us: call_start(): pl.pallas_call(start_kernel, out_shape=outs, in_specs=[vmem] * 8, out_spe...]
    all_to_all x4 -> x1, waiting for transfers between devices: 141 us -> 0.01 us  [fast_body(): ga = lax.all_to_all(ga.reshape(span, -1, 384), 'expert', 0, 0, tiled=True)]
    reduce_scatter x4 -> x5, waiting for transfers between devices: 296 us -> 182 us  [the longest x1 83.2 us: fast_body(): lax.psum_scatter(ge, 'dp', scatter_dimension=1, tiled=True).astype(f32)]
    all_gather x2 -> x0, blocking collectives: 91.2 us -> none  [the longest x1 59 us: body(): lax.all_gather(doc_ids[0].astype(jnp.bfloat16), 'expert', axis=0, tiled=T...]
    dot_general x30 -> x12, matrix products: 65.7 us -> 23.5 us  [the longest x2 4.87 us: fast_body(): inward = jnp.einsum('td,tf->df', h2, dgu[e], preferred_element_type=f32)]
    gather x4 -> x0, local copies, waits for them, and re-layouts: 23.6 us -> none  [the longest x1 8.18 us: body(): back_rows[places].reshape(row_count, TOP, D).astype(jnp.float32)]
    all_to_all x4 -> x1, starting transfers between devices: 25.2 us -> 5.36 us  [fast_body(): ga = lax.all_to_all(ga.reshape(span, -1, 384), 'expert', 0, 0, tiled=True)]
    all_gather x4 -> x1, waiting for transfers between devices: 37.2 us -> 22.7 us  [fast_body(): da = lax.all_gather(dr.astype(bf16), 'expert', axis=0, tiled=True)]
  transfers between devices with their start and end apart: 13 -> 8, of which waited for: 9 -> 7; matrix products, arithmetic and copies ran while one was open for 12% -> 9% of each run, Pallas kernels for 0% -> 0%
where the time goes in v1:
time: 657 us; the launch traced here: 645 us
  waiting for transfers between devices  302 us (46%)
  Pallas kernels  163 us (25%)
  other arithmetic  47.4 us (7%)
  blocking collectives  40.6 us (6%)
  local copies, waits for them, and re-layouts  37.8 us (6%)
  matrix products  28.9 us (4%)
  between operations  19.5 us (3%)
    pallas_call x1, Pallas kernels, call_start(): pl.pallas_call(start_kernel, out_shape=outs, in_specs=[vmem] * 8, out_spe...  138 us
    unnamed x8, waiting for transfers between devices  97 us
    reduce_scatter x1, waiting for transfers between devices, fast_body(): lax.psum_scatter(ge, 'dp', scatter_dimension=1, tiled=True).astype(f32)  83.2 us
    psum x1, blocking collectives, fast_body(): grad_norm = jnp.sqrt(lax.psum(squares, ('dp', 'expert')))  40.6 us
    reduce_scatter x1, waiting for transfers between devices, fast_body(): lax.psum_scatter(d_part.astype(bf16), 'expert', scatter_dimension=0, tile...  32 us
    reduce_scatter x1, waiting for transfers between devices, fast_body(): lax.psum_scatter(y_part.astype(bf16), 'expert', scatter_dimension=0, tile...  31.5 us
    unnamed x67, local copies, waits for them, and re-layouts  26.4 us
    pallas_call x1, Pallas kernels, call_experts(): pl.pallas_call(expert_kernel, out_shape=outs, in_specs=[vmem] * 4, out_sp...  24.9 us
  transfers between devices with their start and end apart: 8, of which 7 were waited for; matrix products, arithmetic and copies ran while one was open for 9% of the time, Pallas kernels for 0%

profile of v1, /device:TPU:24, one launch (start us, length us, event | category | flops | bytes accessed | tf_op | source)
XLA Modules:
  0.0 644.9 jit_solution(10863708559218170176)
XLA Ops:
  7.2 1.0 convert_element_type.86
  11.7 3.2 convert_element_type.87.we_ref
  15.2 2.1 negate_select_fusion
  17.9 1.9 maximum_maximum_fusion
  19.9 138.1 %start.1 = (bf16[8,128,1024]{2,1,0:T(8,128)(2,1)}, bf16[8,128,1024]{2,1,0:T(8,128)(2,1)}, bf16[8,128,1024]{2,1,0:T(8,128)(2,1)}, bf16[1024,256]{1,0:T(8,128)(2,1...) custom-call(bf16[128,1024]{1,0:T(8,128)(2,1)} %bitcast.155, ...), custom_call_target="tpu_custom_call" | custom-call | tf_op jit(solution)/shard_map/start/pallas_call | solution.py:750
  158.0 24.9 %experts.1 = (bf16[1024,1024]{1,0:T(8,128)(2,1)}, bf16[1024,1024]{1,0:T(8,128)(2,1)}, bf16[2,1024,512]{2,1,0:T(8,128)(2,1)}, bf16[2,1024,1024]{2,1,0:T(8,128)(2,1)}) custom-call(bf16[1024,1024]{1,0:T(8,128)(2,1)} %get-tuple-element.29.h2_ref, bf16[1024,1024]{1,0:T(8,128)(2,1)} %bitcast.153, bf16[2,4,256,1536]{3,2,1,0:T(8,128)(2,1)} %get-tuple-element.31.we_ref, ...), custom_call_target="tpu_custom_call" | custom-call | tf_op jit(solution)/shard_map/experts/pallas_call | solution.py:812
  184.0 32.0 %reduce-scatter.11.cloned.1.call-done = bf16[128,1024]{1,0:T(8,128)(2,1)} async-done(((bf16[1024,1024]{1,0:T(8,128)(2,1)}), bf16[128,1024]{1,0:T(8,128)(2,1)}) %reduce-scatter.11.cloned.1.call-update) | async-done | bytes 262160 | tf_op jit(solution)/shard_map/reduce_scatter | solution.py:891
  216.1 1.1 fusion.46
  217.2 1.8 fusion.81
  221.5 5.4 fusion.91
  226.8 22.7 %all-gather.2.cloned.1.call-done = bf16[1024,1024]{1,0:T(8,128)(2,1)} async-done(((bf16[128,1024]{1,0:T(8,128)(2,1)}), bf16[1024,1024]{1,0:T(8,128)(2,1)}) %all-gather.2.cloned.1.call-update) | async-done | bytes 2097168 | tf_op jit(solution)/shard_map/all_gather | solution.py:897
  249.6 2.6 convolution_convert_fusion.5
  252.2 4.8 fusion.1
  257.1 1.2 fusion.29
  258.3 2.5 fusion.3
  260.8 1.2 fusion.32
  263.9 1.2 fusion.35
  265.9 2.0 convolution_convert_fusion
  268.3 2.0 fusion.5
  270.3 1.3 convolution_convert_fusion.2
  271.9 1.2 copy-done.22
  273.1 2.4 fusion.23
  275.9 1.2 copy-done.6
  279.9 3.3 convolution_convert_fusion.1
  283.7 2.5 fusion.26
  286.2 2.0 maximum_bitcast_fusion.1
  288.2 12.7 %reduce-scatter.13.cloned.1.call-done = bf16[128,1024]{1,0:T(8,128)(2,1)} async-done(((bf16[1024,1024]{1,0:T(8,128)(2,1)}), bf16[128,1024]{1,0:T(8,128)(2,1)}) %reduce-scatter.13.cloned.1.call-update) | async-done | bytes 262160 | tf_op jit(solution)/shard_map/reduce_scatter | solution.py:912
  300.8 1.7 fusion.47
  302.6 1.0 copy.213
  303.7 5.1 pad_maximum_fusion
  309.6 22.8 %reduce-scatter.15.cloned.1.call-done = bf16[256,384]{0,1:T(8,128)(2,1)} async-done(((bf16[1024,384]{0,1:T(8,128)(2,1)}), bf16[256,384]{0,1:T(8,128)(2,1)}) %reduce-scatter.15.cloned.1.call-update) | async-done | bytes 196624 | tf_op jit(solution)/shard_map/reduce_scatter | solution.py:917
  332.3 1.7 copy.187
  334.1 5.4 all-to-all-start
  339.4 2.4 copy.195
  342.6 3.6 copy.192
  346.1 3.5 copy.193
  349.7 1.6 multiply_reduce_fusion.1
  356.6 96.2 %reduce-scatter.19.cloned.1.call-done = f32[32,2]{1,0:T(8,128)} async-done(((f32[1024,2]{1,0:T(8,128)}), f32[32,2]{1,0:T(8,128)}) %reduce-scatter.19.cloned.1.call-update) | async-done | bytes 272
  455.5 83.2 %reduce-scatter.17.cloned.1.call-done = bf16[2,256,1536]{1,2,0:T(8,128)(2,1)} async-done(((bf16[2,1024,1536]{1,2,0:T(8,128)(2,1)}), bf16[2,256,1536]{1,2,0:T(8,128)(2,1)}) %reduce-scatter.17.cloned.1.call-update) | async-done | bytes 1572880 | tf_op jit(solution)/shard_map/reduce_scatter | solution.py:921
  538.7 2.8 fusion.15
  542.2 31.5 %reduce-scatter.9.cloned.1.call-done = bf16[128,1024]{1,0:T(8,128)(2,1)} async-done(((bf16[1024,1024]{1,0:T(8,128)(2,1)}), bf16[128,1024]{1,0:T(8,128)(2,1)}) %reduce-scatter.9.cloned.1.call-update) | async-done | bytes 262160 | tf_op jit(solution)/shard_map/reduce_scatter | solution.py:890
  573.6 2.5 fusion.50
  576.1 40.6 %psum.7 = f32[]{:T(128)} all-reduce(f32[]{:T(128)S(6)} %add.125), channel_id=1, replica_groups=mesh['dp'=4,'expert'=8] {'dp','expert'}, use_global_device_ids=true, to_apply=%region_19.20 | all-reduce | flops 1 | bytes 8 | tf_op jit(solution)/shard_map/psum | solution.py:926
  617.4 6.6 %multiply_subtract_fusion = (f32[2,256,1536]{1,2,0:T(8,128)}, f32[2,256,1536]{1,2,0:T(8,128)}, f32[2,256,1536]{1,2,0:T(8,128)}) fusion(f32[2,256,1536]{1,2,0:T(8,128)S(1)} %copy.195, f32[]{:T(128)S(6)} %sub.51, f32[]{:T(128)S(6)} %sub.50, f32[]{:T(128)S(6)} %min.3, bf16[2,256,1536]{1,2,0:T(8,128)(2,1)} %reduce-scatter.17.cloned.1.call-done, ...), kind=kLoop, calls=%fused_computation.31 | loop fusion | flops 13369344 | bytes 20447244 | tf_op jit(solution)/shard_map/sub | solution.py:61
  624.0 3.5 copy.196
  627.5 3.7 copy.197
  631.3 2.4 copy.198
  634.2 2.4 multiply_subtract_fusion.1
  (135 shorter events, 22.7 us)
Async XLA Ops:
  7.2 208.9 %reduce-scatter.11.cloned.1.call-start = ((), (), s32[]{:S(2)}) async-start(), calls=%async_computation.8 | async-start | bytes 2359296 | tf_op jit(solution)/shard_map/reduce_scatter | solution.py:891
  8.9 6.0 copy-start.16
  8.9 6.0 copy-start.17
  158.0 25.0 %copy-start.1 = (f32[128,1024]{1,0:T(8,128)S(1)}, f32[128,1024]{1,0:T(8,128)}, u32[]{:S(2)}) copy-start(f32[128,1024]{1,0:T(8,128)} %get-tuple-element.28) | copy-start | bytes 1572868
  182.9 34.3 %copy-start.5 = (bf16[1,128,1024]{2,1,0:T(8,128)(2,1)S(1)}, bf16[1,128,1024]{2,1,0:T(8,128)(2,1)}, u32[]{:S(2)}) copy-start(bf16[1,128,1024]{2,1,0:T(8,128)(2,1)} %param.19) | copy-start | bytes 786436
  182.9 37.0 %copy-start.13 = (bf16[1024,256]{1,0:T(8,128)(2,1)S(1)}, bf16[1024,256]{1,0:T(8,128)(2,1)}, u32[]{:S(2)}) copy-start(bf16[1024,256]{1,0:T(8,128)(2,1)} %get-tuple-element.36) | copy-start | bytes 1572868
  182.9 37.2 %copy-start.3 = (f32[1024,128]{1,0:T(8,128)S(1)}, f32[1024,128]{1,0:T(8,128)}, u32[]{:S(2)}) copy-start(f32[1024,128]{1,0:T(8,128)} %get-tuple-element.32.cols_ref) | copy-start | bytes 1572868
  182.9 66.7 %all-gather.2.cloned.1.call-start = ((), (), s32[]{:S(2)}) async-start(), calls=%async_computation.9 | async-start | bytes 2359296 | tf_op jit(solution)/shard_map/all_gather | solution.py:897
  217.2 9.6 %copy-start.18 = (f32[128]{0:T(128)}, f32[128]{0:T(128)S(1)}, u32[]{:S(2)}) copy-start(f32[128]{0:T(128)S(1)} %multiply_multiply_fusion.4) | copy-start | bytes 1540
  219.1 81.7 %reduce-scatter.13.cloned.1.call-start = ((), (), s32[]{:S(2)}) async-start(), calls=%async_computation.10 | async-start | bytes 2359296 | tf_op jit(solution)/shard_map/reduce_scatter | solution.py:912
  249.6 7.4 %slice-start = ((s8[8388608]{0:T(1024)(128)(4,1)}), s8[4194304]{0:T(1024)(128)(4,1)S(1)}, s32[]{:S(2)}) async-start(s8[8388608]{0:T(1024)(128)(4,1)} %bitcast.151), calls=%async_computation.14 | async-start | bytes 8388608
  252.2 4.9 slice-start.1
  260.8 1.3 copy-start.14
  263.9 2.0 copy-start.12
  265.1 0.8 copy-start.7
  265.1 3.1 copy-start.4
  265.1 3.2 copy-start.2
  267.9 64.4 %reduce-scatter.15.cloned.1.call-start = ((), (), s32[]{:S(2)}) async-start(), calls=%async_computation.11 | async-start | bytes 983040 | tf_op jit(solution)/shard_map/reduce_scatter | solution.py:917
  268.3 2.0 copy-start.24
  270.3 1.6 copy-start.9
  270.3 2.8 copy-start.22
  275.5 1.6 copy-start.6
  275.5 1.6 copy-start.26
  275.9 1.8 copy-start.8
  275.9 2.2 copy-start.25
  279.8 173.0 %reduce-scatter.19.cloned.1.call-start = ((), (), s32[]{:S(2)}) async-start(), calls=%async_computation.13 | async-start | bytes 540672
  279.9 21.0 %copy-start.19 = (f32[128]{0:T(128)}, f32[128]{0:T(128)S(1)}, u32[]{:S(2)}) copy-start(f32[128]{0:T(128)S(1)} %fusion.78) | copy-start | bytes 1540
  279.9 3.4 copy-start.10
  279.9 3.9 copy-start.23
  303.6 235.1 %reduce-scatter.17.cloned.1.call-start = ((), (), s32[]{:S(2)}) async-start(), calls=%async_computation.12 | async-start | bytes 7864320 | tf_op jit(solution)/shard_map/reduce_scatter | solution.py:921
  308.8 264.8 %reduce-scatter.9.cloned.1.call-start = ((), (), s32[]{:S(2)}) async-start(), calls=%async_computation.7 | async-start | bytes 2359296 | tf_op jit(solution)/shard_map/reduce_scatter | solution.py:890
  334.1 17.2 %all-to-all-start = ((bf16[8,32,384]{2,1,0:T(8,128)(2,1)}), bf16[8,32,384]{2,1,0:T(8,128)(2,1)}, u32[]{:S(2)}, u32[]{:S(2)}) async-start(bf16[8,32,384]{2,1,0:T(8,128)(2,1)} %bitcast.41), calls=%async_computation.5 | async-start | bytes 393216 | tf_op jit(solution)/shard_map/all_to_all | solution.py:919
  627.5 3.7 copy-start
  631.2 2.4 copy-start.15
  631.2 2.4 copy-start.20
  631.2 2.4 copy-start.21
  631.2 3.0 copy-start.11
Sparse Core Ops, SparseCore 0:
  183.1 32.9 reduce-scatter.10
  219.2 30.3 all-gather.1
  268.0 32.7 reduce-scatter.12
  303.6 28.7 reduce-scatter.14
  335.0 117.7 reduce-scatter.18
  455.9 82.7 reduce-scatter.16
  541.7 31.9 reduce-scatter.8

commit v2 on v0

--- a/solution.py
+++ b/solution.py
@@ -2,6 +2,11 @@
 import jax.numpy as jnp
 from jax import lax
 from jax.sharding import PartitionSpec as P
+import types
+
+import numpy as np
+from jax.experimental import pallas as pl
+from jax.experimental.pallas import tpu as pltpu
 
 D = 1024
 H = 16
@@ -88,7 +93,7 @@
     return (gate_up, activated)
 
 
-def body(
+def general_body(
     activations,
     doc_ids,
     routes,
@@ -389,6 +394,901 @@
     )
 
 
+def fits(mesh):
+    return dict(mesh.shape) == {"dp": 4, "expert": KVH}
+
+
+def head_tables(length):
+    halves = np.arange(HD // 2, dtype=np.float32)
+    inverse = np.power(np.float32(ROPE_BASE), np.float32(-2.0) * halves / np.float32(HD))
+    angles = np.arange(length, dtype=np.float32)[:, None] * inverse[None, :]
+    cosine, sine = np.cos(angles), np.sin(angles)
+    cosine = np.concatenate([cosine] * 4, axis=1)
+    return jnp.asarray(cosine), jnp.asarray(np.concatenate([-sine, sine] * 2, axis=1))
+
+
+LINE, SPAN, PLANE, PARTS = 4, 8, 4, 4
+QUERY_BLOCK = 256
+NN, NT, TN = ((1,), (0,)), ((1,), (1,)), ((0,), (0,))
+
+
+def remote(source, target, sent, landed, device):
+    return pltpu.make_async_remote_copy(
+        src_ref=source,
+        dst_ref=target,
+        send_sem=sent,
+        recv_sem=landed,
+        device_id=device,
+        device_id_type=pl.DeviceIdType.MESH,
+    )
+
+
+def whereabouts():
+    i, e = lax.axis_index("dp"), lax.axis_index("expert")
+    return i, e, e // 2, lax.rem(e, 2)
+
+
+def partners(i, e):
+    others = [(i, lax.rem(e + k, SPAN)) for k in range(1, SPAN)]
+    return others + [(lax.rem(i + k, PLANE), e) for k in range(1, PLANE)]
+
+
+def piece(j, size):
+    return pl.ds(pl.multiple_of(j * size, size), size)
+
+
+class LineGather:
+    def __init__(self, slot, source, where, sems):
+        self.slot, self.source, self.where = slot, source, where
+        self.sent, self.passed, self.landed = sems
+
+    def _own(self, j, k):
+        i, e, z, c = self.where
+        there = z * 2 + 1 - c if k == 0 else lax.rem(z + k, LINE) * 2 + c
+        return remote(self.source(j), self.slot(e, j), self.sent.at[j, k], self.landed.at[j, e], (i, there))
+
+    def _pass(self, j, k):
+        i, e, z, c = self.where
+        index = lax.rem(z + k, LINE) * 2 + c
+        place = self.slot(index, j)
+        return remote(place, place, self.passed.at[j, k], self.landed.at[j, index], (i, z * 2 + 1 - c))
+
+    def _relay(self, j):
+        i, e, z, c = self.where
+        index = lax.rem(z + 2, LINE) * 2 + c
+        place = self.slot(index, j)
+        end = LINE - 1 - lax.rem(z + 2, LINE)
+        return remote(place, place, self.passed.at[j, 0], self.landed.at[j, index], (i, end * 2 + c))
+
+    def _each_own(self, j, act):
+        z = self.where[2]
+        act(self._own(j, 2))
+        pl.when(z != LINE - 1)(lambda: act(self._own(j, 1)))
+        pl.when(z != 0)(lambda: act(self._own(j, 3)))
+        act(self._own(j, 0))
+
+    def _when_inner(self, act):
+        z = self.where[2]
+        pl.when((z > 0) & (z < LINE - 1))(act)
+
+    def start(self, j):
+        self._each_own(j, lambda copy: copy.start())
+
+    def wait(self, j, index):
+        i, e, z, c = self.where
+        place = self.slot(index, j)
+        remote(place, place, self.sent.at[j, 0], self.landed.at[j, index], (i, z * 2 + 1 - c)).wait_recv()
+
+    def sibling(self):
+        _, e, z, c = self.where
+        return z * 2 + 1 - c
+
+    def near(self, k):
+        _, e, z, c = self.where
+        return lax.rem(z + k, LINE) * 2 + c
+
+    def far(self, k):
+        _, e, z, c = self.where
+        return lax.rem(z + k, LINE) * 2 + 1 - c
+
+    def forward(self, j, k):
+        self.wait(j, self.near(k))
+        if k == 2:
+            self._when_inner(lambda: self._relay(j).start())
+        self._pass(j, k).start()
+
+    def forward_all(self, j):
+        for k in (2, 1, 3):
+            self.forward(j, k)
+
+    def rest(self, j):
+        self.wait(j, self.sibling())
+        for k in range(1, LINE):
+            self.wait(j, self.far(k))
+
+    def drain(self, j):
+        self._each_own(j, lambda copy: copy.wait_send())
+        self._when_inner(lambda: self._relay(j).wait_send())
+        for k in range(1, LINE):
+            self._pass(j, k).wait_send()
+
+
+class LineScatter:
+    def __init__(self, data, where, pair, out, inbox, own, sems, size):
+        self.data, self.where, self.size = data, where, size
+        self.pair, self.out, self.inbox, self.own = pair, out, inbox, own
+        self.pair_sent, self.pair_landed, self.sent, self.landed = sems
+
+    def _pair(self, j, k):
+        i, e, z, c = self.where
+        there, rows = lax.rem(z + k, LINE), piece(j, self.size)
+        return remote(
+            self.data.at[there * 2 + 1 - c, rows], self.pair.at[there, rows],
+            self.pair_sent.at[j, there], self.pair_landed.at[j, there], (i, z * 2 + 1 - c),
+        )
+
+    def _send(self, j, k):
+        i, e, z, c = self.where
+        there, rows = lax.rem(z + k, LINE), piece(j, self.size)
+        crossing = {1: z // (LINE - 1), 2: 0, 3: (LINE - 1 - z) // (LINE - 1)}[k]
+        chip = {1: z + 1 - 2 * crossing, 2: there, 3: z - 1 + 2 * crossing}[k]
+        slot = z + crossing * (chip - z)
+        return remote(
+            self.out.at[there, rows], self.inbox.at[slot, rows],
+            self.sent.at[j, there], self.landed.at[j, slot], (i, chip * 2 + c),
+        )
+
+    def _landed(self, j, slot):
+        i, e, z, c = self.where
+        place = self.inbox.at[slot, piece(j, self.size)]
+        remote(place, place, self.sent.at[j, slot], self.landed.at[j, slot], (i, z * 2 + 1 - c)).wait_recv()
+
+    def _both(self, j, there):
+        c, rows = self.where[3], piece(j, self.size)
+        return self.data[there * 2 + c, rows].astype(jnp.float32) + self.pair[there, rows].astype(jnp.float32)
+
+    def _across(self, j):
+        there, rows = lax.rem(self.where[2] + 2, LINE), piece(j, self.size)
+        return there, rows, self._both(j, there)
+
+    def start(self, j):
+        for k in (1, 3, 2, 0):
+            self._pair(j, k).start()
+
+    def start_one(self, j, k):
+        self._pair(j, k).start()
+
+    def fold_one(self, j, k):
+        z, rows = self.where[2], piece(j, self.size)
+        self._pair(j, k).wait_recv()
+
+        def send():
+            there = lax.rem(z + k, LINE)
+            self.out[there, rows] = self._both(j, there).astype(jnp.bfloat16)
+            self._send(j, k).start()
+
+        if k == 0:
+            self.own[rows] = self._both(j, z)
+        elif k == 2:
+            pl.when((z == 0) | (z == LINE - 1))(send)
+        else:
+            send()
+
+    def fold(self, j):
+        for k in (1, 3, 2, 0):
+            self.fold_one(j, k)
+
+    def fold_late(self, j):
+        z = self.where[2]
+
+        @pl.when((z > 0) & (z < LINE - 1))
+        def _():
+            there, rows, both = self._across(j)
+            self._landed(j, z)
+            self.out[there, rows] = (both + self.inbox[z, rows].astype(jnp.float32)).astype(jnp.bfloat16)
+            self._send(j, 2).start()
+
+    def total(self, j):
+        z, rows = self.where[2], piece(j, self.size)
+
+        def add(k):
+            there = lax.rem(z + k, LINE)
+            self._landed(j, there)
+            self.own[rows] += self.inbox[there, rows].astype(jnp.float32)
+
+        pl.when(z != LINE - 1)(lambda: add(1))
+        pl.when(z != 0)(lambda: add(3))
+        add(2)
+        return self.own[rows]
+
+    def drain(self, j):
+        for k in range(LINE):
+            self._pair(j, k).wait_send()
+        for k in range(1, LINE):
+            self._send(j, k).wait_send()
+
+
+class PlaneGather:
+    def __init__(self, where, held, sems):
+        i, self.e = where[0], where[1]
+        self.i, self.held, self.sems = i, held, sems
+        self.x = i // 2 * 2 + 1 - lax.rem(i, 2)
+        self.y = (1 - i // 2) * 2 + lax.rem(i, 2)
+        self.far = PLANE - 1 - i
+        self.half = held.shape[2] // 2
+
+    def _copy(self, l, n, source):
+        rows = (slice(None), slice(None), slice(0, self.half), slice(self.half, None))[n]
+        to = (self.x, self.y, self.y, self.x)[n]
+        sent, landed = self.sems
+        place = self.held.at[l, source, rows]
+        return remote(place, place, sent.at[l, n], landed.at[l, n], (to, self.e))
+
+    def start(self, l):
+        self._copy(l, 0, self.i).start()
+        self._copy(l, 1, self.i).start()
+
+    def forward(self, l):
+        self._copy(l, 0, self.x).wait_recv()
+        self._copy(l, 2, self.x).start()
+        self._copy(l, 1, self.y).wait_recv()
+        self._copy(l, 3, self.y).start()
+
+    def rest(self, l):
+        self._copy(l, 2, self.far).wait_recv()
+        self._copy(l, 3, self.far).wait_recv()
+
+    def drain(self, l):
+        for n, source in enumerate((self.i, self.i, self.x, self.y)):
+            self._copy(l, n, source).wait_send()
+
+
+class PlaneScatter:
+    def __init__(self, plane, out, inbox, sems):
+        self.plane, self.out, self.inbox = plane, out, inbox
+        self.sent, self.landed = sems
+        self.half = plane.half
+
+    def _copy(self, l, chunk, part, n):
+        first = slice(0, self.half) if part == 0 else slice(self.half, None)
+        to_x = chunk == 1 or (chunk == 0 and part == 0)
+        return remote(
+            self.out.at[l, chunk, first], self.inbox.at[l, chunk, first], self.sent.at[l, n], self.landed.at[l, n],
+            (self.plane.x if to_x else self.plane.y, self.plane.e),
+        )
+
+    def _at(self, l, chunk, part):
+        return self._copy(l, chunk, part, chunk * 2 + part)
+
+    def start(self, l, chunk):
+        for part in ((0, 1), (0,), (1,))[chunk]:
+            self._at(l, chunk, part).start()
+
+    def combine(self, l):
+        for chunk, part in ((1, 1), (2, 0)):
+            rows = slice(part * self.half, (part + 1) * self.half)
+            self._at(l, 0, part).wait_recv()
+            mine = self.out[l, chunk, rows].astype(jnp.float32) + self.inbox[l, 0, rows].astype(jnp.float32)
+            self.out[l, chunk, rows] = mine.astype(jnp.bfloat16)
+            self._at(l, chunk, part).start()
+
+    def rest(self, l):
+        for chunk in (1, 2):
+            for part in (0, 1):
+                self._at(l, chunk, part).wait_recv()
+
+    def drain(self, l):
+        for chunk in range(3):
+            for part in (0, 1):
+                self._at(l, chunk, part).wait_send()
+
+
+def half_turn_tile(part):
+    lane = lax.broadcasted_iota(jnp.int32, part.shape, 1)
+    ahead = pltpu.roll(part, 128 - HD // 2, 1)
+    behind = pltpu.roll(part, HD // 2, 1)
+    return jnp.where(lax.rem(lane, HD) < HD // 2, ahead, behind)
+
+
+def rms_rows(values):
+    return lax.rsqrt(jnp.mean(values * values, axis=-1, keepdims=True) + EPSILON)
+
+
+def norm_back(values, gain, upper):
+    scale = rms_rows(values)
+    scaled = upper * gain
+    inner = jnp.mean(values * scaled, axis=-1, keepdims=True)
+    return scale * scaled - values * (scale * scale * scale) * inner, upper * values * scale
+
+
+def dot(a, b, contract):
+    return lax.dot_general(a, b, (contract, ((), ())), preferred_element_type=jnp.float32)
+
+
+def visible_keys(first, low, high, docs_row, docs_col):
+    shape = (QUERY_BLOCK, high - low)
+    key = lax.broadcasted_iota(jnp.int32, shape, 1) + low
+    query = lax.broadcasted_iota(jnp.int32, shape, 0) + first
+    return (key <= query) & (docs_row[:, low:high] == docs_col)
+
+
+def layer_kernel(x, up, wa, we, routes, gates, doc_ids, shard_gains, cos, sin, block, grad, norm, ge, ga, gn, **held):
+    layer_body(
+        types.SimpleNamespace(
+            x=x, up=up, wa=wa, we=we, routes=routes, gates=gates, doc_ids=doc_ids, shard_gains=shard_gains,
+            cos=cos, sin=sin,
+            block=block, grad=grad, norm=norm, ge=ge, ga=ga, gn=gn, **held,
+        )
+    )
+
+
+def layer_outputs(rows, local):
+    f32 = jnp.float32
+    shaped = jax.ShapeDtypeStruct
+    deep = D // PLANE
+    return [
+        shaped((rows, D), jnp.bfloat16), shaped((rows, D), f32), shaped((8, 128), f32),
+        shaped((local, deep, 3 * FF), f32), shaped((deep // SPAN, 3072), f32), shaped((8, rows), f32),
+    ]
+
+
+def layer_scratch(rows, local):
+    f32, bf16 = jnp.float32, jnp.bfloat16
+    held, sems = pltpu.VMEM, lambda *shape: pltpu.SemaphoreType.DMA(shape)
+    deep = D // PLANE
+    part = deep // SPAN
+    blocks = held((SPAN, rows, D), bf16)
+    quarter = held((LINE, rows, D), bf16)
+    line = lambda parts: (sems(parts, LINE), sems(parts, LINE), sems(parts, SPAN))
+    scatter = lambda parts: tuple(sems(parts, LINE) for _ in range(4))
+    both = lambda *shape: (sems(*shape), sems(*shape))
+    return dict(
+        x_all=blocks, up_all=blocks, h1=blocks, o_all=blocks, h2=blocks, d=blocks, da_all=blocks,
+        qkv=held((SPAN * rows, 256), bf16), lse=held((SPAN * rows, 128), f32),
+        wq_out=held((SPAN, part, 256), bf16), w_mine=held((PLANE, SPAN, part, 256), bf16),
+        wo_all=held((PLANE, LINE, 2, part, D), bf16), we_all=held((local, PLANE, deep, 3 * FF), bf16),
+        o_own=held((SPAN, rows, 128), bf16),
+        r_part=held((SPAN, rows // PARTS, D), f32), r_own=held((rows, D), f32),
+        pack=held((SPAN, 8, rows), f32), pack_all=held((SPAN, 8, rows), f32), gain_sum=held((PLANE, 2, 8, 128), f32),
+        cols=held((SPAN, rows, 128), f32), docs=held((8, SPAN * rows), f32), gains=held((8, D), f32),
+        act=held((local, SPAN, rows, FF), bf16), dgu=held((local, SPAN, rows, 2 * FF), bf16),
+        pair=quarter, out=quarter, inbox=quarter, own=held((rows, D), f32),
+        y_pair=quarter, y_out=quarter, y_inbox=quarter, y_own=held((rows, D), f32),
+        ge_in=held((local, PLANE - 1, deep, 3 * FF), bf16),
+        do=held((SPAN, rows, 128), bf16), dkv=held((SPAN * rows, 128), f32), dqkv=held((SPAN * rows, 256), bf16),
+        dr=held((rows, D), f32), gn_two=held((8, D), f32),
+        ga_out=held((PLANE - 1, deep, 384), bf16), ga_in=held((PLANE - 1, deep, 384), bf16),
+        gs=held((SPAN, part, 384), f32), ga_all=held((SPAN, part, 384), f32),
+        gn_in=held((PLANE, 8, D), f32), mix_in=held((SPAN, 8, D), f32), sq_in=held((PLANE, 8, 128), f32),
+        x_sems=line(1), up_sems=line(PARTS), wo_sems=line(1), o_sems=line(PARTS), da_sems=line(PARTS),
+        d_sems=scatter(PARTS), y_sems=scatter(1), h_sems=scatter(1),
+        load=sems(local), pack_sems=both(SPAN), wq_sems=both(SPAN), wqd_sems=both(PLANE), gd_sems=both(PLANE),
+        wod_sems=both(PLANE), wop_sems=both(PLANE), we_sems=both(local, 4), ge_sems=both(local, 6),
+        ga_sems=both(PLANE), gn_sems=both(PLANE), gs_sems=both(SPAN), mix_sems=both(SPAN), sq_sems=both(PLANE),
+    )
+
+
+def layer_body(v):
+    f32, bf16 = jnp.float32, jnp.bfloat16
+    where = i, e, z, c = whereabouts()
+    sibling = (i, z * 2 + 1 - c)
+    rows, local, deep = v.x.shape[0], v.we_all.shape[0], v.ge.shape[1]
+    length, size = rows * SPAN, rows // PARTS
+    own_cols = piece(e, 128)
+    live = []
+
+    def go(*spec):
+        copy = remote(*spec)
+        copy.start()
+        live.append(copy)
+
+    def along(k):
+        return lax.rem(i + k, PLANE)
+
+    def across(k):
+        return lax.rem(e + k, SPAN)
+
+    def line(sems, slot, source):
+        return LineGather(slot, source, where, sems)
+
+    x_line = line(v.x_sems, lambda s, j: v.x_all.at[s], lambda j: v.x)
+    up_line = line(v.up_sems, lambda s, j: v.up_all.at[s, piece(j, size)], lambda j: v.up.at[piece(j, size)])
+    wo_line = line(
+        v.wo_sems, lambda s, j: v.wo_all.at[i, s // 2, lax.rem(s, 2)], lambda j: v.wo_all.at[i, z, c]
+    )
+    o_line = line(
+        v.o_sems,
+        lambda s, j: v.o_all.at[:, piece(j, size), piece(s, 128)],
+        lambda j: v.o_own.at[:, piece(j, size)],
+    )
+    da_line = line(
+        v.da_sems, lambda s, j: v.da_all.at[s, piece(j, size)], lambda j: v.da_all.at[e, piece(j, size)]
+    )
+    we_plane = PlaneGather(where, v.we_all, v.we_sems)
+    ge_plane = PlaneScatter(we_plane, v.we_all, v.ge_in, v.ge_sems)
+    d_scatter = LineScatter(v.d, where, v.pair, v.out, v.inbox, v.own, v.d_sems, size)
+    y_scatter = LineScatter(v.o_all, where, v.y_pair, v.y_out, v.y_inbox, v.y_own, v.y_sems, rows)
+    h_scatter = LineScatter(v.d, where, v.pair, v.out, v.inbox, v.own, v.h_sems, rows)
+
+    loads = [pltpu.make_async_copy(v.we.at[l], v.ge.at[l], v.load.at[l]) for l in range(local)]
+    for copy in loads:
+        copy.start()
+    barrier = pltpu.get_barrier_semaphore()
+    for device in partners(i, e):
+        pl.semaphore_signal(barrier, inc=1, device_id=device, device_id_type=pl.DeviceIdType.MESH)
+    lane = lax.broadcasted_iota(jnp.int32, (2, rows), 1)
+    index, few = i * SPAN + e, rows // v.shard_gains.shape[1]
+    spread = jnp.concatenate([v.shard_gains[...]] * few, axis=1)
+    spread = jnp.where(lane // (rows // few) == lax.rem(index, few), spread, 0.0)
+    shared = [v.doc_ids[...].astype(f32), spread, jnp.zeros((3, rows), f32)]
+    for g in range(SPAN):
+        named = [
+            jnp.sum(jnp.where(v.routes[...] == g * local + l, v.gates[...], 0.0), axis=0, keepdims=True)
+            for l in range(local)
+        ]
+        v.pack[g] = jnp.concatenate(named + shared, axis=0)
+    for g in range(SPAN):
+        v.wq_out[g, :, :128] = v.wa[:, g * 128 : (g + 1) * 128].astype(bf16)
+        key_value = [v.wa[:, first + g * HD : first + (g + 1) * HD] for first in (QD, QD + KVD)]
+        v.wq_out[g, :, 128:] = jnp.concatenate(key_value, axis=1).astype(bf16)
+    v.w_mine[i, e] = v.wq_out[e]
+    v.wo_all[i, z, c] = v.wa[:, QKV:].astype(bf16)
+    v.pack_all[e] = v.pack[e]
+    v.x_all[e] = v.x[...]
+    v.up_all[e] = v.up[...]
+    pl.semaphore_wait(barrier, SPAN + PLANE - 2)
+    for k in range(1, SPAN):
+        go(v.pack.at[across(k)], v.pack_all.at[e], v.pack_sems[0].at[k], v.pack_sems[1].at[e], (i, across(k)))
+    for k in range(1, SPAN):
+        go(v.wq_out.at[across(k)], v.w_mine.at[i, e], v.wq_sems[0].at[k], v.wq_sems[1].at[e], (i, across(k)))
+    wo_line.start(0)
+    x_line.start(0)
+    loads[0].wait()
+    v.we_all[0, i] = v.ge[0].astype(bf16)
+
+    for k in range(1, SPAN):
+        slot = v.pack_all.at[across(k)]
+        remote(slot, slot, v.pack_sems[0].at[k], v.pack_sems[1].at[across(k)], sibling).wait_recv()
+    for half in range(2):
+        summed = v.pack_all[4 * half]
+        for s in range(1, 4):
+            summed = summed + v.pack_all[4 * half + s]
+        v.gain_sum[i, half] = summed
+    for k in range(1, PLANE):
+        go(v.gain_sum.at[i], v.gain_sum.at[i], v.gd_sems[0].at[k], v.gd_sems[1].at[i], (along(k), e))
+    for k in range(1, SPAN):
+        slot = v.w_mine.at[i, across(k)]
+        remote(slot, slot, v.wq_sems[0].at[k], v.wq_sems[1].at[across(k)], sibling).wait_recv()
+    for k in range(1, PLANE):
+        go(v.w_mine.at[i], v.w_mine.at[i], v.wqd_sems[0].at[k], v.wqd_sems[1].at[i], (along(k), e))
+    we_plane.start(0)
+    loads[1].wait()
+    v.we_all[1, i] = v.ge[1].astype(bf16)
+    for s in range(SPAN):
+        block = v.pack_all[s]
+        tall = jnp.concatenate([block, jnp.zeros((rows - block.shape[0], rows), f32)], axis=0)
+        v.cols[s] = tall.T
+        v.docs[:, s * rows : (s + 1) * rows] = block
+    for k in range(1, PLANE):
+        slot = v.gain_sum.at[along(k)]
+        remote(slot, slot, v.gd_sems[0].at[k], v.gd_sems[1].at[along(k)], sibling).wait_recv()
+    for tile in range(2 * PLANE):
+        v.gains[:, tile * 128 : (tile + 1) * 128] = v.gain_sum[tile // 2, tile % 2].astype(bf16).astype(f32)
+    gain_one, gain_two = v.gains[3:4], v.gains[4:5]
+
+    def first_norm(s):
+        values = v.x_all[s].astype(f32)
+        v.h1[s] = (values * rms_rows(values) * gain_one).astype(bf16)
+
+    wo_line.forward_all(0)
+    for k in range(1, PLANE):
+        mine = v.wo_all.at[i, :, c]
+        go(mine, mine, v.wod_sems[0].at[k], v.wod_sems[1].at[i], (along(k), e))
+    first_norm(e)
+    for k in (2, 1, 3):
+        x_line.forward(0, k)
+        first_norm(x_line.near(k))
+    up_line.start(0)
+    up_line.start(1)
+    we_plane.forward(0)
+    we_plane.start(1)
+    x_line.wait(0, x_line.sibling())
+    first_norm(x_line.sibling())
+    for k in range(1, LINE):
+        x_line.wait(0, x_line.far(k))
+        first_norm(x_line.far(k))
+    for k in range(1, PLANE):
+        slot = v.w_mine.at[along(k)]
+        remote(slot, slot, v.wqd_sems[0].at[k], v.wqd_sems[1].at[along(k)], sibling).wait_recv()
+
+    weights = v.w_mine[...].reshape(D, 256)
+    lane = lax.broadcasted_iota(jnp.int32, (QUERY_BLOCK, 128), 1)
+
+    def tables(first):
+        cosine, sine = v.cos[first : first + QUERY_BLOCK], v.sin[first : first + QUERY_BLOCK]
+        return cosine, sine, jnp.where(lane < HD, cosine, 1.0), jnp.where(lane < HD, sine, 0.0)
+
+    for first in range(0, length, QUERY_BLOCK):
+        span = slice(first, first + QUERY_BLOCK)
+        slots = slice(first // rows, (first + QUERY_BLOCK) // rows)
+        raw = dot(v.h1[slots].reshape(QUERY_BLOCK, D), weights, NN)
+        q_cos, q_sin, kv_cos, kv_sin = tables(first)
+        q_raw, kv_raw = raw[:, :128], raw[:, 128:]
+        v.qkv[span, :128] = (q_raw * q_cos + half_turn_tile(q_raw) * q_sin).astype(bf16)
+        v.qkv[span, 128:] = (kv_raw * kv_cos + half_turn_tile(kv_raw) * kv_sin).astype(bf16)
+
+
+    def block_masks(first):
+        low, high = max(0, first - length // 2), first + QUERY_BLOCK
+        slots = slice(first // rows, (first + QUERY_BLOCK) // rows)
+        docs_col = v.cols[slots, :, 2:3].reshape(QUERY_BLOCK, 1)
+        return low, high, slots, visible_keys(first, low, high, v.docs[2:3], docs_col)
+
+    for first in range(0, length, QUERY_BLOCK):
+        low, high, slots, visible = block_masks(first)
+        span = slice(first, first + QUERY_BLOCK)
+        outs, logs = [], []
+        for head in range(2):
+            q = v.qkv[span, head * HD : (head + 1) * HD]
+            scores = dot(q, v.qkv[low:high, 128:192], NT) * HD**-0.5
+            scores = jnp.where(visible, scores, -1e30)
+            peak = jnp.max(scores, axis=-1, keepdims=True)
+            raw = jnp.exp(scores - peak)
+            total = jnp.sum(raw, axis=-1, keepdims=True)
+            probs = raw * (1.0 / total)
+            logs.append(peak + jnp.log(total))
+            outs.append(dot(probs.astype(bf16), v.qkv[low:high, 192:256], NN))
+        both = jnp.concatenate(outs, axis=1).astype(bf16).reshape(-1, rows, 128)
+        v.o_own[slots] = both
+        v.o_all[slots, :, own_cols] = both
+        v.lse[span] = jnp.where(lane == 0, logs[0], logs[1])
+    o_line.start(0)
+    o_line.start(1)
+    up_line.start(2)
+    o_line.start(2)
+    up_line.start(3)
+    o_line.start(3)
+
+    wo_line.rest(0)
+    for k in range(1, PLANE):
+        here = v.wo_all.at[along(k), :, c]
+        remote(here, here, v.wod_sems[0].at[k], v.wod_sems[1].at[along(k)], sibling).wait_recv()
+        go(here, here, v.wop_sems[0].at[k], v.wop_sems[1].at[along(k)], sibling)
+    for k in range(1, PLANE):
+        far = v.wo_all.at[along(k), :, 1 - c]
+        remote(far, far, v.wod_sems[0].at[k], v.wop_sems[1].at[along(k)], sibling).wait_recv()
+
+    def second_norm(j):
+        part = piece(j, size)
+        w_out = v.wo_all[...].reshape(D, D)
+        branch = dot(v.o_all[:, part].reshape(-1, D), w_out, NT)
+        values = v.x_all[:, part].reshape(-1, D).astype(f32) + branch
+        v.r_part[...] = values.reshape(SPAN, size, D)
+        v.r_own[part] = v.r_part[e]
+        v.h2[:, part] = (values * rms_rows(values) * gain_two).astype(bf16).reshape(SPAN, size, D)
+
+    def gate_of(l, part):
+        return v.cols[:, part, l : l + 1].reshape(-1, 1)
+
+    def expert(l, j):
+        part = piece(j, size)
+        weights = v.we_all[l].reshape(D, 3 * FF)
+        gate = gate_of(l, part)
+        routed = gate > 0
+        gu = dot(v.h2[:, part].reshape(-1, D), weights[:, : 2 * FF], NN)
+        g, u = gu[:, :FF], gu[:, FF:]
+        sig = 1.0 / (1.0 + jnp.exp(-g))
+        act = jnp.where(routed, g * sig * u, 0.0).astype(bf16)
+        v.act[l, :, part] = act.reshape(SPAN, size, FF)
+        dy = (gate * v.up_all[:, part].reshape(-1, D).astype(f32)).astype(bf16)
+        dact = dot(dy, weights[:, 2 * FF :], NN)
+        dg = dact * u * sig * (1.0 + g * (1.0 - sig))
+        du = dact * g * sig
+        dgu = jnp.where(routed, jnp.concatenate([dg, du], axis=1), 0.0).astype(bf16)
+        v.dgu[l, :, part] = dgu.reshape(SPAN, size, 2 * FF)
+        d = dot(dgu, weights[:, : 2 * FF], NT).astype(bf16)
+        y = dot(act, weights[:, 2 * FF :], NT).astype(bf16)
+        if l == 0:
+            v.d[:, part] = d.reshape(SPAN, size, D)
+            v.o_all[:, part] = y.reshape(SPAN, size, D)
+        else:
+            d = v.d[:, part].reshape(-1, D).astype(f32) + d.astype(f32)
+            v.d[:, part] = d.astype(bf16).reshape(SPAN, size, D)
+            y = gate_of(0, part) * v.o_all[:, part].reshape(-1, D).astype(f32) + gate * y.astype(f32)
+            v.o_all[:, part] = y.astype(bf16).reshape(SPAN, size, D)
+
+    we_plane.rest(0)
+
+    def first_round(j, carry):
+        @pl.when(j == PARTS - 1)
+        def _():
+            we_plane.forward(1)
+
+        @pl.when(j < PARTS)
+        def _():
+            o_line.forward_all(j)
+            up_line.forward_all(j)
+
+        @pl.when(j > 0)
+        def _():
+            o_line.drain(j - 1)
+            expert(0, j - 1)
+
+        @pl.when(j < PARTS)
+        def _():
+            o_line.rest(j)
+            up_line.rest(j)
+            second_norm(j)
+
+        return carry
+
+    lax.fori_loop(0, PARTS + 1, first_round, 0)
+    we_plane.rest(1)
+
+    def second_round(j, carry):
+        @pl.when(j < PARTS)
+        def _():
+            expert(1, j)
+            d_scatter.start(j)
+
+        @pl.when((j > 0) & (j <= PARTS))
+        def _():
+            d_scatter.fold(j - 1)
+
+        @pl.when(j > 1)
+        def _():
+            d_scatter.fold_late(j - 2)
+
+        return carry
+
+    lax.fori_loop(0, PARTS + 2, second_round, 0)
+    y_scatter.start(0)
+    for l in range(local):
+        we_plane.drain(l)
+
+    def expert_chunk(l, there):
+        span = piece(there, deep)
+        inward = dot(v.h2[:, :, span].reshape(length, deep), v.dgu[l].reshape(length, 2 * FF), TN)
+        gate = v.cols[:, :, l : l + 1].reshape(length, 1)
+        dy = (gate * v.up_all[:, :, span].reshape(length, deep).astype(f32)).astype(bf16)
+        return inward, dot(dy, v.act[l].reshape(length, FF), TN)
+
+    def send_chunk(l, chunk):
+        inward, down = expert_chunk(l, (we_plane.far, we_plane.x, we_plane.y)[chunk])
+        v.we_all[l, chunk, :, : 2 * FF] = inward.astype(bf16)
+        v.we_all[l, chunk, :, 2 * FF :] = down.astype(bf16)
+        ge_plane.start(l, chunk)
+
+    def keep_chunk(l):
+        inward, down = expert_chunk(l, i)
+        v.ge[l, :, : 2 * FF] = inward
+        v.ge[l, :, 2 * FF :] = down
+
+    v.gn_two[...] = jnp.zeros_like(v.gn_two)
+
+    def second_back(j):
+        part = piece(j, size)
+        back, shares = norm_back(v.r_own[part], gain_two, d_scatter.total(j))
+        dr = v.up_all[e, part].astype(f32) + back
+        v.dr[part] = dr
+        v.gn_two[:1] += jnp.sum(shares, axis=0, keepdims=True)
+        v.da_all[e, part] = dr.astype(bf16)
+        da_line.start(j)
+
+    send_chunk(0, 0)
+    send_chunk(1, 0)
+    second_back(0)
+    send_chunk(0, 1)
+    send_chunk(0, 2)
+    second_back(1)
+    ge_plane.combine(0)
+    send_chunk(1, 1)
+    second_back(2)
+    send_chunk(1, 2)
+    ge_plane.combine(1)
+    second_back(3)
+    keep_chunk(0)
+    keep_chunk(1)
+    y_scatter.fold(0)
+    wo_mine = v.wo_all[:, :, :, :, own_cols].reshape(D, 128)
+    for j in range(PARTS):
+        da_line.forward_all(j)
+    y_scatter.fold_late(0)
+    for j in range(PARTS):
+        da_line.rest(j)
+        part = piece(j, size)
+        do = dot(v.da_all[:, part].reshape(-1, D), wo_mine, NN).astype(bf16)
+        v.do[:, part] = do.reshape(SPAN, size, 128)
+
+    v.dkv[...] = jnp.zeros_like(v.dkv)
+    for first in range(0, length, QUERY_BLOCK):
+        low, high, slots, visible = block_masks(first)
+        span = slice(first, first + QUERY_BLOCK)
+        keys, values = v.qkv[low:high, 128:192], v.qkv[low:high, 192:256]
+        do_both = v.do[slots].reshape(QUERY_BLOCK, 128)
+        dqs, dk, dv = [], 0.0, 0.0
+        for head in range(2):
+            q = v.qkv[span, head * HD : (head + 1) * HD]
+            do = do_both[:, head * HD : (head + 1) * HD]
+            scores = dot(q, keys, NT) * HD**-0.5
+            probs = jnp.exp(jnp.where(visible, scores - v.lse[span, head : head + 1], -1e30))
+            dp = dot(do, values, NT)
+            delta = jnp.sum(probs * dp, axis=-1, keepdims=True)
+            ds = (probs * (dp - delta)).astype(bf16)
+            dqs.append(dot(ds, keys, NN))
+            dk = dk + dot(ds, q, TN)
+            dv = dv + dot(probs.astype(bf16), do, TN)
+        v.dkv[low:high] += jnp.concatenate([dk * HD**-0.5, dv], axis=1)
+        dq = jnp.concatenate(dqs, axis=1) * HD**-0.5
+        cosine, sine = v.cos[span], v.sin[span]
+        v.dqkv[span, :128] = (dq * cosine - half_turn_tile(dq) * sine).astype(bf16)
+    for first in range(0, length, QUERY_BLOCK):
+        span = slice(first, first + QUERY_BLOCK)
+        dkv = v.dkv[span]
+        _, _, cosine, sine = tables(first)
+        v.dqkv[span, 128:] = (dkv * cosine - half_turn_tile(dkv) * sine).astype(bf16)
+
+    o = v.o_own[...].reshape(length, 128)
+    dqkv = v.dqkv[...]
+
+    def rows_copy(k):
+        return remote(v.ga_out.at[k - 1], v.ga_in.at[k - 1], v.ga_sems[0].at[k], v.ga_sems[1].at[k], (along(k), e))
+
+    for k in (2, 1, 3, 0):
+        span = piece(along(k), deep)
+        projections = dot(v.h1[:, :, span].reshape(length, deep), dqkv, TN)
+        output = dot(v.da_all[:, :, span].reshape(length, deep), o, TN)
+        if k == 0:
+            v.gs[:, :, :256] = projections.reshape(SPAN, -1, 256)
+            v.gs[:, :, 256:] = output.reshape(SPAN, -1, 128)
+        else:
+            v.ga_out[k - 1, :, :256] = projections.astype(bf16)
+            v.ga_out[k - 1, :, 256:] = output.astype(bf16)
+            rows_copy(k).start()
+
+    for j in range(PARTS):
+        d_scatter.drain(j)
+    gn_one = jnp.zeros((1, D), f32)
+    order = (1, 3, 2, 0)
+    for n, k in enumerate(order):
+        chip = lax.rem(z + k, LINE)
+        slots = piece(chip, 2)
+        dh = dot(v.dqkv[piece(chip, 2 * rows)], weights, NT)
+        values = v.x_all[slots].reshape(2 * rows, D).astype(f32)
+        gn_one = gn_one + jnp.sum(dh * values * rms_rows(values), axis=0, keepdims=True)
+        v.d[slots] = dh.astype(bf16).reshape(2, rows, D)
+        h_scatter.start_one(0, k)
+        if n > 0:
+            h_scatter.fold_one(0, order[n - 1])
+    h_scatter.fold_one(0, order[-1])
+    v.gn_in[i] = jnp.concatenate([gn_one, v.gn_two[:1], jnp.zeros((6, D), f32)], axis=0)
+    for k in range(1, PLANE):
+        go(v.gn_in.at[i], v.gn_in.at[i], v.gn_sems[0].at[k], v.gn_sems[1].at[i], (along(k), e))
+    v.block[...] = (v.r_own[...] + y_scatter.total(0)).astype(bf16)
+    h_scatter.fold_late(0)
+
+    for k in (2, 1, 3):
+        rows_copy(k).wait_recv()
+        v.gs[...] += v.ga_in[k - 1].reshape(v.gs.shape).astype(f32)
+    squares = jnp.sum(v.gs[...] * v.gs[...])
+    for k in range(1, SPAN):
+        go(v.gs.at[across(k)], v.ga_all.at[e], v.gs_sems[0].at[k], v.gs_sems[1].at[e], (i, across(k)))
+    v.ga_all[e] = v.gs[e]
+    for l in range(local):
+        ge_plane.rest(l)
+        for first in range(0, deep, 64):
+            span = slice(first, first + 64)
+            summed = v.ge[l, span]
+            for chunk in (1, 2):
+                summed = summed + v.ge_in[l, chunk, span].astype(f32)
+            v.ge[l, span] = summed
+            squares = squares + jnp.sum(summed * summed)
+
+    for k in range(1, PLANE):
+        slot = v.gn_in.at[along(k)]
+        remote(slot, slot, v.gn_sems[0].at[k], v.gn_sems[1].at[along(k)], sibling).wait_recv()
+    gains = v.gn_in[0] + v.gn_in[1] + v.gn_in[2] + v.gn_in[3]
+    row = lax.broadcasted_iota(jnp.int32, gains.shape, 0)
+    v.mix_in[e] = jnp.where(row == 2, squares, gains)
+    for k in range(1, SPAN):
+        go(v.mix_in.at[e], v.mix_in.at[e], v.mix_sems[0].at[k], v.mix_sems[1].at[e], (i, across(k)))
+    for k in range(1, SPAN):
+        slot = v.mix_in.at[across(k)]
+        remote(slot, slot, v.mix_sems[0].at[k], v.mix_sems[1].at[across(k)], sibling).wait_recv()
+    mixed = v.mix_in[0]
+    for s in range(1, SPAN):
+        mixed = mixed + v.mix_in[s]
+    v.gains[...] = mixed
+    turned = pltpu.roll(v.gains[:, piece(index // few, rows)], rows - lax.rem(index, few) * (rows // few), 1)
+    v.gn[...] = turned
+    v.sq_in[i] = jnp.broadcast_to(mixed[2:3, :128], (8, 128))
+    for k in range(1, PLANE):
+        go(v.sq_in.at[i], v.sq_in.at[i], v.sq_sems[0].at[k], v.sq_sems[1].at[i], (along(k), e))
+    gain_squares = jnp.sum(jnp.where(row < 2, mixed * mixed, 0.0))
+    for k in range(1, SPAN):
+        slot = v.ga_all.at[across(k)]
+        remote(slot, slot, v.gs_sems[0].at[k], v.gs_sems[1].at[across(k)], sibling).wait_recv()
+    for g in range(SPAN):
+        v.ga[:, g * 128 : (g + 1) * 128] = v.ga_all[g, :, :128]
+        v.ga[:, QKV + g * 128 : QKV + (g + 1) * 128] = v.ga_all[g, :, 256:]
+    for g in range(0, SPAN, 2):
+        for first, own in ((QD, 128), (QD + KVD, 192)):
+            heads = [v.ga_all[g + n, :, own : own + HD] for n in range(2)]
+            v.ga[:, first + g * HD : first + (g + 2) * HD] = jnp.concatenate(heads, axis=1)
+    for k in range(1, PLANE):
+        slot = v.sq_in.at[along(k)]
+        remote(slot, slot, v.sq_sems[0].at[k], v.sq_sems[1].at[along(k)], sibling).wait_recv()
+    v.norm[...] = jnp.sqrt(v.sq_in[0] + v.sq_in[1] + v.sq_in[2] + v.sq_in[3] + gain_squares)
+
+    back, _ = norm_back(v.x_all[e].astype(f32), gain_one, h_scatter.total(0))
+    v.grad[...] = v.dr[...] + back
+    for copy in live:
+        copy.wait_send()
+    for k in (2, 1, 3):
+        rows_copy(k).wait_send()
+    for l in range(local):
+        ge_plane.drain(l)
+    for item in (x_line, wo_line, y_scatter, h_scatter):
+        item.drain(0)
+    for j in range(PARTS):
+        up_line.drain(j)
+        da_line.drain(j)
+
+
+def call_layer(*args):
+    vmem, anywhere = pl.BlockSpec(memory_space=pltpu.VMEM), pl.BlockSpec(memory_space=pl.ANY)
+    rows, local = args[0].shape[0], args[3].shape[0]
+    outs = layer_outputs(rows, local)
+    return pl.pallas_call(
+        layer_kernel,
+        out_shape=outs,
+        in_specs=[anywhere if n == 3 else vmem for n in range(len(args))],
+        out_specs=[vmem] * len(outs),
+        scratch_shapes=layer_scratch(rows, local),
+        compiler_params=pltpu.CompilerParams(
+            collective_id=0, has_side_effects=True, vmem_limit_bytes=64 * 2**20 - 2**18
+        ),
+        name="layer",
+    )(*args)
+
+
+def fast_body(
+    activations,
+    doc_ids,
+    routes,
+    gate_weights,
+    cotangent,
+    step_count,
+    w_attn,
+    norm_gains,
+    w_expert,
+    first_attn,
+    second_attn,
+    first_gains,
+    second_gains,
+    first_expert,
+    second_expert,
+):
+    cosine, sine = head_tables(activations.shape[1] * lax.axis_size("expert"))
+    block, input_total, norm, grad_expert, grad_attn, gn = call_layer(
+        activations[0], cotangent[0], w_attn, w_expert, routes[0].T, gate_weights[0].T, doc_ids, norm_gains.T,
+        cosine, sine,
+    )
+    grad_norm = norm[0, 0]
+    clip = jnp.minimum(1.0, CLIP_NORM / (grad_norm + 1e-06))
+    steps = step_count.astype(jnp.float32)
+    attn = adam_update(
+        w_attn, first_attn, second_attn, grad_attn * clip, steps, WEIGHT_DECAY, LEARN_RATE
+    )
+    gain = adam_update(
+        norm_gains.T, first_gains.T, second_gains.T, gn[:2, : norm_gains.shape[0]] * clip, steps, 0.0, GAIN_RATE
+    )
+    expert = adam_update(
+        w_expert, first_expert, second_expert, grad_expert * clip, steps, WEIGHT_DECAY, LEARN_RATE
+    )
+    return (block[None], input_total[None], grad_norm, *attn, *[a.T for a in gain], *expert)
+
+
 def solution(mesh):
     in_specs = (
         P("dp", "expert", None),
@@ -421,4 +1321,5 @@
         P("expert", "dp", None),
         P("expert", "dp", None),
     )
+    body = fast_body if fits(mesh) else general_body
     return jax.shard_map(body, mesh=mesh, in_specs=in_specs, out_specs=out_specs, check_vma=False)

time: 989 us -> 219 us (0.22); the launches traced: 977 us -> 218 us
  waiting for transfers between devices: 572 us -> 0 us
  Pallas kernels: 0 us -> 203 us
  blocking collectives: 130 us -> 0 us
  local copies, waits for them, and re-layouts: 101 us -> 2.74 us
  matrix products: 65.7 us -> 0 us
  other arithmetic: 62.1 us -> 10.9 us
  starting transfers between devices: 25.7 us -> 0 us
  between operations: 19.7 us -> 2.18 us
    reduce_scatter x4 -> x0, waiting for transfers between devices: 296 us -> none  [the longest x1 159 us: body(): lax.psum_scatter(attn_partial, ('dp', 'expert'), scatter_dimension=0, til...]
    pallas_call x0 -> x1, Pallas kernels: none -> 203 us  [call_layer(): pl.pallas_call(layer_kernel, out_shape=outs, in_specs=[anywhere if n == 3...]
    all_to_all x4 -> x0, waiting for transfers between devices: 141 us -> none  [the longest x2 92.4 us: to_sender(): lax.all_to_all(buffer, 'expert', split_axis=1, concat_axis=0, tiled=True)]
    unnamed x10 -> x0, waiting for transfers between devices: 97.3 us -> none
    all_gather x2 -> x0, blocking collectives: 91.2 us -> none  [the longest x1 59 us: body(): lax.all_gather(doc_ids[0].astype(jnp.bfloat16), 'expert', axis=0, tiled=T...]
    dot_general x30 -> x0, matrix products: 65.7 us -> none  [the longest x2 6.61 us: output_step(): jnp.einsum('grtk,kgd->tgrd', weights_low, value_part(block_id), preferred...]
    psum x1 -> x0, blocking collectives: 39.2 us -> none  [body(): grad_norm = jnp.sqrt(lax.psum(local_squares, ('dp', 'expert')))]
    all_gather x4 -> x0, waiting for transfers between devices: 37.2 us -> none  [the longest x1 37.1 us: attn_fetch(): lax.all_gather(w_attn.astype(jnp.bfloat16), ('dp', 'expert'), axis=0, til...]
  transfers between devices with their start and end apart: 13 -> 0, of which waited for: 9 -> 0; matrix products, arithmetic and copies ran while one was open for 12% -> 0% of each run, Pallas kernels for 0% -> 0%
where the time goes in v2:
time: 219 us; the launch traced here: 218 us
  Pallas kernels  203 us (93%)
  other arithmetic  10.9 us (5%)
  local copies, waits for them, and re-layouts  2.74 us (1%)
    pallas_call x1, Pallas kernels, call_layer(): pl.pallas_call(layer_kernel, out_shape=outs, in_specs=[anywhere if n == 3...  203 us
    sub x2, other arithmetic, adam_update(): weight - step_rate * (first_hat / (jnp.sqrt(second_hat) + ADAM_EPSILON) +...  9.57 us

profile of v2, /device:TPU:24, one launch (start us, length us, event | category | flops | bytes accessed | tf_op | source)
XLA Modules:
  0.0 218.5 jit_solution(5452524019191401073)
XLA Ops:
  0.6 202.7 %layer.1 = (bf16[128,1024]{1,0:T(8,128)(2,1)}, f32[128,1024]{1,0:T(8,128)}, f32[8,128]{1,0:T(8,128)}, f32[2,256,1536]{2,1,0:T(8,128)}, f32[32,3072]{1,0:T(8,128)}, /*index=5*/f32[8,128]{1,0:T(8,128)}) custom-call(bf16[128,1024]{1,0:T(8,128)(2,1)} %bitcast.32, bf16[128,1024]{1,0:T(8,128)(2,1)} %bitcast.33, f32[32,3072]{1,0:T(8,128)} %wa.1, ...), custom_call_target="tpu_custom_call" | custom-call | tf_op jit(solution)/shard_map/layer/pallas_call | solution.py:1242
  203.3 1.2 slice.6
  205.9 0.0 copy-start.6
  205.9 0.0 copy-start.7
  206.0 0.0 copy-start.8
  206.0 0.0 copy-start
  206.0 0.0 copy-start.2
  206.0 0.0 copy-start.3
  206.0 0.0 copy-start.4
  206.0 0.0 copy-start.5
  206.0 8.4 %multiply_subtract_fusion = (f32[2,256,1536]{2,1,0:T(8,128)}, f32[2,256,1536]{2,1,0:T(8,128)}, f32[2,256,1536]{2,1,0:T(8,128)}) fusion(f32[2,256,1536]{2,1,0:T(8,128)} %we.1, f32[]{:T(128)S(6)} %sub.20, f32[]{:T(128)S(6)} %sub.19, f32[2,256,1536]{2,1,0:T(8,128)} %get-tuple-element.23, f32[]{:T(128)S(6)} %min.3, f32[2,256,1536]{2,1,0:T(8,128)} %param.31, ...), kind=kLoop, calls=%fused_computation.2 | loop fusion | flops 12582912 | bytes 22020108 | tf_op jit(solution)/shard_map/sub | solution.py:63
  214.4 0.0 copy-start.1
  214.4 0.0 copy-done.6
  214.4 0.0 copy-done.7
  214.4 0.0 copy-done.8
  214.4 1.3 fusion.4
  215.7 0.0 copy-done
  215.7 0.0 copy-done.2
  215.8 0.0 copy-done.3
  215.8 0.0 copy-done.4
  215.8 1.2 multiply_subtract_fusion.1
  217.0 0.0 copy-done.5
  217.0 0.7 copy.32
  217.7 0.0 copy-done.1
  217.7 0.8 copy.33
Async XLA Ops:
  205.9 8.5 %copy-start.6 = (f32[32,2]{0,1:T(2,128)S(1)}, f32[32,2]{0,1:T(2,128)}, u32[]{:S(2)}) copy-start(f32[32,2]{0,1:T(2,128)} %param.24) | copy-start | bytes 772
  205.9 8.5 %copy-start.7 = (f32[32,2]{0,1:T(2,128)S(1)}, f32[32,2]{0,1:T(2,128)}, u32[]{:S(2)}) copy-start(f32[32,2]{0,1:T(2,128)} %param.29) | copy-start | bytes 772
  206.0 8.5 %copy-start.8 = (f32[32,2]{0,1:T(2,128)S(1)}, f32[32,2]{0,1:T(2,128)}, u32[]{:S(2)}) copy-start(f32[32,2]{0,1:T(2,128)} %param.28) | copy-start | bytes 772
  206.0 9.8 %copy-start = (f32[32,3072]{1,0:T(8,128)S(1)}, f32[32,3072]{1,0:T(8,128)}, u32[]{:S(2)}) copy-start(f32[32,3072]{1,0:T(8,128)} %wa.1) | copy-start | bytes 1179652
  206.0 9.8 %copy-start.2 = (f32[32,3072]{1,0:T(8,128)S(1)}, f32[32,3072]{1,0:T(8,128)}, u32[]{:S(2)}) copy-start(f32[32,3072]{1,0:T(8,128)} %param.27) | copy-start | bytes 1179652
  206.0 9.8 %copy-start.3 = (f32[32,3072]{1,0:T(8,128)S(1)}, f32[32,3072]{1,0:T(8,128)}, u32[]{:S(2)}) copy-start(f32[32,3072]{1,0:T(8,128)} %param.26) | copy-start | bytes 1179652
  206.0 9.8 %copy-start.4 = (f32[32,3072]{1,0:T(8,128)S(1)}, f32[32,3072]{1,0:T(8,128)}, u32[]{:S(2)}) copy-start(f32[32,3072]{1,0:T(8,128)} %get-tuple-element.21) | copy-start | bytes 1179652
  206.0 11.0 %copy-start.5 = (bf16[128,1024]{1,0:T(8,128)(2,1)S(1)}, bf16[128,1024]{1,0:T(8,128)(2,1)}, u32[]{:S(2)}) copy-start(bf16[128,1024]{1,0:T(8,128)(2,1)} %get-tuple-element.18) | copy-start | bytes 786436
  214.4 3.3 %copy-start.1 = (f32[128,1024]{1,0:T(8,128)S(1)}, f32[128,1024]{1,0:T(8,128)}, u32[]{:S(2)}) copy-start(f32[128,1024]{1,0:T(8,128)} %get-tuple-element.19) | copy-start | bytes 1572868

commit v3 on v2

--- a/solution.py
+++ b/solution.py
@@ -712,12 +712,12 @@
     return (key <= query) & (docs_row[:, low:high] == docs_col)
 
 
-def layer_kernel(x, up, wa, we, routes, gates, doc_ids, shard_gains, cos, sin, block, grad, norm, ge, ga, gn, **held):
+def layer_kernel(x, up, wa, we, routes, gates, doc_ids, shard_gains, cos, sin, block, grad, norm, ge_far, ga, gn, clip, **held):
     layer_body(
         types.SimpleNamespace(
             x=x, up=up, wa=wa, we=we, routes=routes, gates=gates, doc_ids=doc_ids, shard_gains=shard_gains,
             cos=cos, sin=sin,
-            block=block, grad=grad, norm=norm, ge=ge, ga=ga, gn=gn, **held,
+            block=block, grad=grad, norm=norm, ge_far=ge_far, ga=ga, gn=gn, clip=clip, **held,
         )
     )
 
@@ -727,8 +727,9 @@
     shaped = jax.ShapeDtypeStruct
     deep = D // PLANE
     return [
-        shaped((rows, D), jnp.bfloat16), shaped((rows, D), f32), shaped((8, 128), f32),
+        shaped((rows, D), jnp.bfloat16), shaped((rows, D), f32), shaped((1, 1), f32),
         shaped((local, deep, 3 * FF), f32), shaped((deep // SPAN, 3072), f32), shaped((8, rows), f32),
+        shaped((1, 1), f32),
     ]
 
 
@@ -758,8 +759,9 @@
         do=held((SPAN, rows, 128), bf16), dkv=held((SPAN * rows, 128), f32), dqkv=held((SPAN * rows, 256), bf16),
         dr=held((rows, D), f32), gn_two=held((8, D), f32),
         ga_out=held((PLANE - 1, deep, 384), bf16), ga_in=held((PLANE - 1, deep, 384), bf16),
-        gs=held((SPAN, part, 384), f32), ga_all=held((SPAN, part, 384), f32),
-        gn_in=held((PLANE, 8, D), f32), mix_in=held((SPAN, 8, D), f32), sq_in=held((PLANE, 8, 128), f32),
+        gs=held((SPAN, part, 384), f32), gs_out=held((SPAN, part, 384), bf16), ga_all=held((SPAN, part, 384), bf16),
+        gn_in=held((PLANE, 16, 128), f32), mix_in=held((SPAN, 24, 128), f32), sq_in=held((PLANE, 8, 128), f32),
+        ge=held((local, deep, 3 * FF), f32), store=sems(local),
         x_sems=line(1), up_sems=line(PARTS), wo_sems=line(1), o_sems=line(PARTS), da_sems=line(PARTS),
         d_sems=scatter(PARTS), y_sems=scatter(1), h_sems=scatter(1),
         load=sems(local), pack_sems=both(SPAN), wq_sems=both(SPAN), wqd_sems=both(PLANE), gd_sems=both(PLANE),
@@ -813,6 +815,7 @@
     loads = [pltpu.make_async_copy(v.we.at[l], v.ge.at[l], v.load.at[l]) for l in range(local)]
     for copy in loads:
         copy.start()
+    results = [pltpu.make_async_copy(v.ge.at[l], v.ge_far.at[l], v.store.at[l]) for l in range(local)]
     barrier = pltpu.get_barrier_semaphore()
     for device in partners(i, e):
         pl.semaphore_signal(barrier, inc=1, device_id=device, device_id_type=pl.DeviceIdType.MESH)
@@ -845,6 +848,7 @@
     x_line.start(0)
     loads[0].wait()
     v.we_all[0, i] = v.ge[0].astype(bf16)
+    we_plane.start(0)
 
     for k in range(1, SPAN):
         slot = v.pack_all.at[across(k)]
@@ -861,7 +865,6 @@
         remote(slot, slot, v.wq_sems[0].at[k], v.wq_sems[1].at[across(k)], sibling).wait_recv()
     for k in range(1, PLANE):
         go(v.w_mine.at[i], v.w_mine.at[i], v.wqd_sems[0].at[k], v.wqd_sems[1].at[i], (along(k), e))
-    we_plane.start(0)
     loads[1].wait()
     v.we_all[1, i] = v.ge[1].astype(bf16)
     for s in range(SPAN):
@@ -1025,27 +1028,6 @@
     lax.fori_loop(0, PARTS + 1, first_round, 0)
     we_plane.rest(1)
 
-    def second_round(j, carry):
-        @pl.when(j < PARTS)
-        def _():
-            expert(1, j)
-            d_scatter.start(j)
-
-        @pl.when((j > 0) & (j <= PARTS))
-        def _():
-            d_scatter.fold(j - 1)
-
-        @pl.when(j > 1)
-        def _():
-            d_scatter.fold_late(j - 2)
-
-        return carry
-
-    lax.fori_loop(0, PARTS + 2, second_round, 0)
-    y_scatter.start(0)
-    for l in range(local):
-        we_plane.drain(l)
-
     def expert_chunk(l, there):
         span = piece(there, deep)
         inward = dot(v.h2[:, :, span].reshape(length, deep), v.dgu[l].reshape(length, 2 * FF), TN)
@@ -1058,6 +1040,31 @@
         v.we_all[l, chunk, :, : 2 * FF] = inward.astype(bf16)
         v.we_all[l, chunk, :, 2 * FF :] = down.astype(bf16)
         ge_plane.start(l, chunk)
+
+    we_plane.drain(0)
+
+    def second_round(j, carry):
+        @pl.when(j < PARTS)
+        def _():
+            expert(1, j)
+            d_scatter.start(j)
+
+        for chunk in range(3):
+            pl.when(j == chunk)(lambda chunk=chunk: send_chunk(0, chunk))
+
+        @pl.when((j > 0) & (j <= PARTS))
+        def _():
+            d_scatter.fold(j - 1)
+
+        @pl.when(j > 1)
+        def _():
+            d_scatter.fold_late(j - 2)
+
+        return carry
+
+    lax.fori_loop(0, PARTS + 2, second_round, 0)
+    y_scatter.start(0)
+    we_plane.drain(1)
 
     def keep_chunk(l):
         inward, down = expert_chunk(l, i)
@@ -1075,16 +1082,13 @@
         v.da_all[e, part] = dr.astype(bf16)
         da_line.start(j)
 
-    send_chunk(0, 0)
     send_chunk(1, 0)
     second_back(0)
-    send_chunk(0, 1)
-    send_chunk(0, 2)
-    second_back(1)
     ge_plane.combine(0)
     send_chunk(1, 1)
+    second_back(1)
+    send_chunk(1, 2)
     second_back(2)
-    send_chunk(1, 2)
     ge_plane.combine(1)
     second_back(3)
     keep_chunk(0)
@@ -1161,7 +1165,8 @@
         if n > 0:
             h_scatter.fold_one(0, order[n - 1])
     h_scatter.fold_one(0, order[-1])
-    v.gn_in[i] = jnp.concatenate([gn_one, v.gn_two[:1], jnp.zeros((6, D), f32)], axis=0)
+    both_gains = jnp.concatenate([gn_one, v.gn_two[:1]], axis=0)
+    v.gn_in[i] = jnp.concatenate([both_gains[:, t : t + 128] for t in range(0, D, 128)], axis=0)
     for k in range(1, PLANE):
         go(v.gn_in.at[i], v.gn_in.at[i], v.gn_sems[0].at[k], v.gn_sems[1].at[i], (along(k), e))
     v.block[...] = (v.r_own[...] + y_scatter.total(0)).astype(bf16)
@@ -1171,9 +1176,8 @@
         rows_copy(k).wait_recv()
         v.gs[...] += v.ga_in[k - 1].reshape(v.gs.shape).astype(f32)
     squares = jnp.sum(v.gs[...] * v.gs[...])
-    for k in range(1, SPAN):
-        go(v.gs.at[across(k)], v.ga_all.at[e], v.gs_sems[0].at[k], v.gs_sems[1].at[e], (i, across(k)))
-    v.ga_all[e] = v.gs[e]
+    v.gs_out[...] = v.gs[...].astype(bf16)
+    v.ga_all[e] = v.gs_out[e]
     for l in range(local):
         ge_plane.rest(l)
         for first in range(0, deep, 64):
@@ -1183,45 +1187,52 @@
                 summed = summed + v.ge_in[l, chunk, span].astype(f32)
             v.ge[l, span] = summed
             squares = squares + jnp.sum(summed * summed)
+        results[l].start()
 
     for k in range(1, PLANE):
         slot = v.gn_in.at[along(k)]
         remote(slot, slot, v.gn_sems[0].at[k], v.gn_sems[1].at[along(k)], sibling).wait_recv()
     gains = v.gn_in[0] + v.gn_in[1] + v.gn_in[2] + v.gn_in[3]
-    row = lax.broadcasted_iota(jnp.int32, gains.shape, 0)
-    v.mix_in[e] = jnp.where(row == 2, squares, gains)
+    v.mix_in[e] = jnp.concatenate([gains, jnp.full((8, 128), squares)], axis=0)
     for k in range(1, SPAN):
         go(v.mix_in.at[e], v.mix_in.at[e], v.mix_sems[0].at[k], v.mix_sems[1].at[e], (i, across(k)))
+    for k in range(1, SPAN):
+        go(v.gs_out.at[across(k)], v.ga_all.at[e], v.gs_sems[0].at[k], v.gs_sems[1].at[e], (i, across(k)))
     for k in range(1, SPAN):
         slot = v.mix_in.at[across(k)]
         remote(slot, slot, v.mix_sems[0].at[k], v.mix_sems[1].at[across(k)], sibling).wait_recv()
     mixed = v.mix_in[0]
     for s in range(1, SPAN):
         mixed = mixed + v.mix_in[s]
-    v.gains[...] = mixed
-    turned = pltpu.roll(v.gains[:, piece(index // few, rows)], rows - lax.rem(index, few) * (rows // few), 1)
-    v.gn[...] = turned
-    v.sq_in[i] = jnp.broadcast_to(mixed[2:3, :128], (8, 128))
+    v.sq_in[i] = mixed[16:]
     for k in range(1, PLANE):
         go(v.sq_in.at[i], v.sq_in.at[i], v.sq_sems[0].at[k], v.sq_sems[1].at[i], (along(k), e))
-    gain_squares = jnp.sum(jnp.where(row < 2, mixed * mixed, 0.0))
+    gain_squares = jnp.sum(mixed[:16] * mixed[:16])
+    row = lax.broadcasted_iota(jnp.int32, (16, 128), 0)
+    pick = lambda n: jnp.sum(jnp.where(row == index // few * 2 + n, mixed[:16], 0.0), axis=0, keepdims=True)
+    own_gains = jnp.concatenate([pick(0), pick(1), jnp.zeros((6, 128), f32)], axis=0)
+    v.gn[...] = pltpu.roll(own_gains, rows - lax.rem(index, few) * (rows // few), 1)
     for k in range(1, SPAN):
         slot = v.ga_all.at[across(k)]
         remote(slot, slot, v.gs_sems[0].at[k], v.gs_sems[1].at[across(k)], sibling).wait_recv()
     for g in range(SPAN):
-        v.ga[:, g * 128 : (g + 1) * 128] = v.ga_all[g, :, :128]
-        v.ga[:, QKV + g * 128 : QKV + (g + 1) * 128] = v.ga_all[g, :, 256:]
+        v.ga[:, g * 128 : (g + 1) * 128] = v.ga_all[g, :, :128].astype(f32)
+        v.ga[:, QKV + g * 128 : QKV + (g + 1) * 128] = v.ga_all[g, :, 256:].astype(f32)
     for g in range(0, SPAN, 2):
         for first, own in ((QD, 128), (QD + KVD, 192)):
             heads = [v.ga_all[g + n, :, own : own + HD] for n in range(2)]
-            v.ga[:, first + g * HD : first + (g + 2) * HD] = jnp.concatenate(heads, axis=1)
+            v.ga[:, first + g * HD : first + (g + 2) * HD] = jnp.concatenate(heads, axis=1).astype(f32)
     for k in range(1, PLANE):
         slot = v.sq_in.at[along(k)]
         remote(slot, slot, v.sq_sems[0].at[k], v.sq_sems[1].at[along(k)], sibling).wait_recv()
-    v.norm[...] = jnp.sqrt(v.sq_in[0] + v.sq_in[1] + v.sq_in[2] + v.sq_in[3] + gain_squares)
+    norm = jnp.sqrt(v.sq_in[0] + v.sq_in[1] + v.sq_in[2] + v.sq_in[3] + gain_squares)[:1, :1]
+    v.norm[...] = norm
+    v.clip[...] = jnp.minimum(1.0, CLIP_NORM / (norm + 1e-06))
 
     back, _ = norm_back(v.x_all[e].astype(f32), gain_one, h_scatter.total(0))
     v.grad[...] = v.dr[...] + back
+    for copy in results:
+        copy.wait()
     for copy in live:
         copy.wait_send()
     for k in (2, 1, 3):
@@ -1243,7 +1254,7 @@
         layer_kernel,
         out_shape=outs,
         in_specs=[anywhere if n == 3 else vmem for n in range(len(args))],
-        out_specs=[vmem] * len(outs),
+        out_specs=[anywhere if n == 3 else vmem for n in range(len(outs))],
         scratch_shapes=layer_scratch(rows, local),
         compiler_params=pltpu.CompilerParams(
             collective_id=0, has_side_effects=True, vmem_limit_bytes=64 * 2**20 - 2**18
@@ -1270,12 +1281,11 @@
     second_expert,
 ):
     cosine, sine = head_tables(activations.shape[1] * lax.axis_size("expert"))
-    block, input_total, norm, grad_expert, grad_attn, gn = call_layer(
+    block, input_total, norm, grad_expert, grad_attn, gn, clip = call_layer(
         activations[0], cotangent[0], w_attn, w_expert, routes[0].T, gate_weights[0].T, doc_ids, norm_gains.T,
         cosine, sine,
     )
-    grad_norm = norm[0, 0]
-    clip = jnp.minimum(1.0, CLIP_NORM / (grad_norm + 1e-06))
+    grad_norm = norm.reshape(())
     steps = step_count.astype(jnp.float32)
     attn = adam_update(
         w_attn, first_attn, second_attn, grad_attn * clip, steps, WEIGHT_DECAY, LEARN_RATE
@@ -1284,7 +1294,7 @@
         norm_gains.T, first_gains.T, second_gains.T, gn[:2, : norm_gains.shape[0]] * clip, steps, 0.0, GAIN_RATE
     )
     expert = adam_update(
-        w_expert, first_expert, second_expert, grad_expert * clip, steps, WEIGHT_DECAY, LEARN_RATE
+        w_expert, first_expert, second_expert, grad_expert * clip[None], steps, WEIGHT_DECAY, LEARN_RATE
     )
     return (block[None], input_total[None], grad_norm, *attn, *[a.T for a in gain], *expert)
 

time: 219 us -> 194 us (0.89)
  Pallas kernels: 203 us -> 176 us
    pallas_call x1, Pallas kernels: 203 us -> 176 us  [call_layer(): pl.pallas_call(layer_kernel, out_shape=outs, in_specs=[anywhere if n == 3...]
where the time goes in v3:
time: 194 us
  Pallas kernels  176 us (91%)
  other arithmetic  13 us (7%)
  between operations  3.29 us (2%)
    pallas_call x1, Pallas kernels, call_layer(): pl.pallas_call(layer_kernel, out_shape=outs, in_specs=[anywhere if n == 3...  176 us
    sub x2, other arithmetic, adam_update(): weight - step_rate * (first_hat / (jnp.sqrt(second_hat) + ADAM_EPSILON) +...  10.9 us

profile of v3, /device:TPU:24, one launch (start us, length us, event | category | flops | bytes accessed | tf_op | source)
XLA Modules:
  0.0 193.9 jit_solution(16200734889156634609)
XLA Ops:
  0.6 176.1 %layer.1 = (bf16[128,1024]{1,0:T(8,128)(2,1)}, f32[128,1024]{1,0:T(8,128)}, f32[1,1]{1,0:T(1,128)}, f32[2,256,1536]{2,1,0:T(8,128)}, f32[32,3072]{1,0:T(8,128)}, /*index=5*/f32[8,128]{1,0:T(8,128)}, f32[1,1]{1,0:T(1,128)}) custom-call(bf16[128,1024]{1,0:T(8,128)(2,1)} %bitcast.33, bf16[128,1024]{1,0:T(8,128)(2,1)} %bitcast.34, f32[32,3072]{1,0:T(8,128)} %wa.1, ...), custom_call_target="tpu_custom_call" | custom-call | tf_op jit(solution)/shard_map/layer/pallas_call | solution.py:1253
  177.5 0.0 copy-start.6
  177.5 0.0 copy-start.7
  177.5 0.0 copy-start.8
  177.6 0.0 copy-start
  177.6 0.0 copy-start.2
  177.6 0.0 copy-start.3
  177.6 0.0 copy-start.4
  177.6 0.0 copy-start.5
  177.6 9.1 %multiply_subtract_fusion = (f32[2,256,1536]{2,1,0:T(8,128)}, f32[2,256,1536]{2,1,0:T(8,128)}, f32[2,256,1536]{2,1,0:T(8,128)}) fusion(f32[2,256,1536]{2,1,0:T(8,128)} %we.1, f32[]{:T(128)S(6)} %sub.20, f32[]{:T(128)S(6)} %sub.19, f32[2,256,1536]{2,1,0:T(8,128)} %get-tuple-element.25, f32[]{:T(128)} %bitcast.10, f32[2,256,1536]{2,1,0:T(8,128)} %param.31, ...), kind=kLoop, calls=%fused_computation.2 | loop fusion | flops 12582912 | bytes 22020108 | tf_op jit(solution)/shard_map/sub | solution.py:63
  186.7 0.0 copy-start.1
  186.7 0.0 copy-done.6
  186.7 0.0 copy-done.7
  186.7 0.0 copy-done.8
  186.7 2.0 %fusion.4 = (f32[32,2]{0,1:T(2,128)}, f32[32,2]{0,1:T(2,128)}, f32[32,2]{0,1:T(2,128)}) fusion(f32[]{:T(128)} %bitcast.10, f32[8,128]{1,0:T(8,128)} %get-tuple-element.24, f32[32,2]{0,1:T(2,128)S(1)} %copy-done.7, f32[]{:T(128)S(6)} %sub.20, f32[]{:T(128)S(6)} %sub.19, f32[32,2]{0,1:T(2,128)S(1)} %copy-done.8, f32[32,2]{0,1:T(2,128)S(1)} %copy-done.6), kind=kLoop, calls=%fused_computation.14 | loop fusion | flops 1024 | bytes 1804 | tf_op jit(solution)/shard_map/transpose | solution.py:1299
  188.7 0.0 copy-done
  188.7 0.0 copy-done.2
  188.7 0.0 copy-done.3
  188.7 0.0 copy-done.4
  188.7 1.9 multiply_subtract_fusion.1
  190.6 0.0 copy-done.5
  190.6 0.7 copy.33
  191.3 0.0 copy-done.1
  191.3 0.8 copy.34
Async XLA Ops:
  177.5 9.1 %copy-start.6 = (f32[32,2]{0,1:T(2,128)S(1)}, f32[32,2]{0,1:T(2,128)}, u32[]{:S(2)}) copy-start(f32[32,2]{0,1:T(2,128)} %param.24) | copy-start | bytes 772
  177.5 9.1 %copy-start.7 = (f32[32,2]{0,1:T(2,128)S(1)}, f32[32,2]{0,1:T(2,128)}, u32[]{:S(2)}) copy-start(f32[32,2]{0,1:T(2,128)} %param.29) | copy-start | bytes 772
  177.5 9.1 %copy-start.8 = (f32[32,2]{0,1:T(2,128)S(1)}, f32[32,2]{0,1:T(2,128)}, u32[]{:S(2)}) copy-start(f32[32,2]{0,1:T(2,128)} %param.28) | copy-start | bytes 772
  177.6 11.2 %copy-start = (f32[32,3072]{1,0:T(8,128)S(1)}, f32[32,3072]{1,0:T(8,128)}, u32[]{:S(2)}) copy-start(f32[32,3072]{1,0:T(8,128)} %wa.1) | copy-start | bytes 1179652
  177.6 11.1 %copy-start.2 = (f32[32,3072]{1,0:T(8,128)S(1)}, f32[32,3072]{1,0:T(8,128)}, u32[]{:S(2)}) copy-start(f32[32,3072]{1,0:T(8,128)} %param.27) | copy-start | bytes 1179652
  177.6 11.1 %copy-start.3 = (f32[32,3072]{1,0:T(8,128)S(1)}, f32[32,3072]{1,0:T(8,128)}, u32[]{:S(2)}) copy-start(f32[32,3072]{1,0:T(8,128)} %param.26) | copy-start | bytes 1179652
  177.6 11.1 %copy-start.4 = (f32[32,3072]{1,0:T(8,128)S(1)}, f32[32,3072]{1,0:T(8,128)}, u32[]{:S(2)}) copy-start(f32[32,3072]{1,0:T(8,128)} %get-tuple-element.22) | copy-start | bytes 1179652
  177.6 13.0 %copy-start.5 = (bf16[128,1024]{1,0:T(8,128)(2,1)S(1)}, bf16[128,1024]{1,0:T(8,128)(2,1)}, u32[]{:S(2)}) copy-start(bf16[128,1024]{1,0:T(8,128)(2,1)} %get-tuple-element.19) | copy-start | bytes 786436
  186.7 4.7 %copy-start.1 = (f32[128,1024]{1,0:T(8,128)S(1)}, f32[128,1024]{1,0:T(8,128)}, u32[]{:S(2)}) copy-start(f32[128,1024]{1,0:T(8,128)} %get-tuple-element.20) | copy-start | bytes 1572868

commit v4 on v3

--- a/solution.py
+++ b/solution.py
@@ -609,19 +609,19 @@
 
 
 class PlaneGather:
-    def __init__(self, where, held, sems):
+    def __init__(self, where, slot, size, sems):
         i, self.e = where[0], where[1]
-        self.i, self.held, self.sems = i, held, sems
+        self.i, self.slot, self.sems = i, slot, sems
         self.x = i // 2 * 2 + 1 - lax.rem(i, 2)
         self.y = (1 - i // 2) * 2 + lax.rem(i, 2)
         self.far = PLANE - 1 - i
-        self.half = held.shape[2] // 2
+        self.half = size // 2
 
     def _copy(self, l, n, source):
         rows = (slice(None), slice(None), slice(0, self.half), slice(self.half, None))[n]
         to = (self.x, self.y, self.y, self.x)[n]
         sent, landed = self.sems
-        place = self.held.at[l, source, rows]
+        place = self.slot(l, source, rows)
         return remote(place, place, sent.at[l, n], landed.at[l, n], (to, self.e))
 
     def start(self, l):
@@ -749,7 +749,7 @@
         wq_out=held((SPAN, part, 256), bf16), w_mine=held((PLANE, SPAN, part, 256), bf16),
         wo_all=held((PLANE, LINE, 2, part, D), bf16), we_all=held((local, PLANE, deep, 3 * FF), bf16),
         o_own=held((SPAN, rows, 128), bf16),
-        r_part=held((SPAN, rows // PARTS, D), f32), r_own=held((rows, D), f32),
+        r_own=held((rows, D), f32),
         pack=held((SPAN, 8, rows), f32), pack_all=held((SPAN, 8, rows), f32), gain_sum=held((PLANE, 2, 8, 128), f32),
         cols=held((SPAN, rows, 128), f32), docs=held((8, SPAN * rows), f32), gains=held((8, D), f32),
         act=held((local, SPAN, rows, FF), bf16), dgu=held((local, SPAN, rows, 2 * FF), bf16),
@@ -765,7 +765,7 @@
         x_sems=line(1), up_sems=line(PARTS), wo_sems=line(1), o_sems=line(PARTS), da_sems=line(PARTS),
         d_sems=scatter(PARTS), y_sems=scatter(1), h_sems=scatter(1),
         load=sems(local), pack_sems=both(SPAN), wq_sems=both(SPAN), wqd_sems=both(PLANE), gd_sems=both(PLANE),
-        wod_sems=both(PLANE), wop_sems=both(PLANE), we_sems=both(local, 4), ge_sems=both(local, 6),
+        wod_sems=both(1, 4), wop_sems=both(PLANE), we_sems=both(local, 4), ge_sems=both(local, 6),
         ga_sems=both(PLANE), gn_sems=both(PLANE), gs_sems=both(SPAN), mix_sems=both(SPAN), sq_sems=both(PLANE),
     )
 
@@ -806,7 +806,8 @@
     da_line = line(
         v.da_sems, lambda s, j: v.da_all.at[s, piece(j, size)], lambda j: v.da_all.at[e, piece(j, size)]
     )
-    we_plane = PlaneGather(where, v.we_all, v.we_sems)
+    we_plane = PlaneGather(where, lambda l, s, part: v.we_all.at[l, s, part], deep, v.we_sems)
+    wo_plane = PlaneGather(where, lambda l, s, part: v.wo_all.at[s, part, c], LINE, v.wod_sems)
     ge_plane = PlaneScatter(we_plane, v.we_all, v.ge_in, v.ge_sems)
     d_scatter = LineScatter(v.d, where, v.pair, v.out, v.inbox, v.own, v.d_sems, size)
     y_scatter = LineScatter(v.o_all, where, v.y_pair, v.y_out, v.y_inbox, v.y_own, v.y_sems, rows)
@@ -884,9 +885,7 @@
         v.h1[s] = (values * rms_rows(values) * gain_one).astype(bf16)
 
     wo_line.forward_all(0)
-    for k in range(1, PLANE):
-        mine = v.wo_all.at[i, :, c]
-        go(mine, mine, v.wod_sems[0].at[k], v.wod_sems[1].at[i], (along(k), e))
+    wo_plane.start(0)
     first_norm(e)
     for k in (2, 1, 3):
         x_line.forward(0, k)
@@ -894,7 +893,6 @@
     up_line.start(0)
     up_line.start(1)
     we_plane.forward(0)
-    we_plane.start(1)
     x_line.wait(0, x_line.sibling())
     first_norm(x_line.sibling())
     for k in range(1, LINE):
@@ -951,23 +949,25 @@
     o_line.start(2)
     up_line.start(3)
     o_line.start(3)
+    wo_plane.forward(0)
+    we_plane.start(1)
 
     wo_line.rest(0)
+    wo_plane.rest(0)
     for k in range(1, PLANE):
         here = v.wo_all.at[along(k), :, c]
-        remote(here, here, v.wod_sems[0].at[k], v.wod_sems[1].at[along(k)], sibling).wait_recv()
         go(here, here, v.wop_sems[0].at[k], v.wop_sems[1].at[along(k)], sibling)
     for k in range(1, PLANE):
         far = v.wo_all.at[along(k), :, 1 - c]
-        remote(far, far, v.wod_sems[0].at[k], v.wop_sems[1].at[along(k)], sibling).wait_recv()
+        remote(far, far, v.wop_sems[0].at[k], v.wop_sems[1].at[along(k)], sibling).wait_recv()
 
     def second_norm(j):
         part = piece(j, size)
         w_out = v.wo_all[...].reshape(D, D)
         branch = dot(v.o_all[:, part].reshape(-1, D), w_out, NT)
         values = v.x_all[:, part].reshape(-1, D).astype(f32) + branch
-        v.r_part[...] = values.reshape(SPAN, size, D)
-        v.r_own[part] = v.r_part[e]
+        split = values.reshape(SPAN, size, D)
+        v.r_own[part] = sum(jnp.where(e == s, split[s], 0.0) for s in range(SPAN))
         v.h2[:, part] = (values * rms_rows(values) * gain_two).astype(bf16).reshape(SPAN, size, D)
 
     def gate_of(l, part):
@@ -1041,13 +1041,15 @@
         v.we_all[l, chunk, :, 2 * FF :] = down.astype(bf16)
         ge_plane.start(l, chunk)
 
-    we_plane.drain(0)
-
     def second_round(j, carry):
         @pl.when(j < PARTS)
         def _():
             expert(1, j)
             d_scatter.start(j)
+
+        @pl.when(j == 0)
+        def _():
+            we_plane.drain(0)
 
         for chunk in range(3):
             pl.when(j == chunk)(lambda chunk=chunk: send_chunk(0, chunk))
@@ -1091,13 +1093,14 @@
     second_back(2)
     ge_plane.combine(1)
     second_back(3)
+    da_line.forward_all(0)
+    da_line.forward_all(1)
     keep_chunk(0)
+    da_line.forward_all(2)
     keep_chunk(1)
+    da_line.forward_all(3)
     y_scatter.fold(0)
     wo_mine = v.wo_all[:, :, :, :, own_cols].reshape(D, 128)
-    for j in range(PARTS):
-        da_line.forward_all(j)
-    y_scatter.fold_late(0)
     for j in range(PARTS):
         da_line.rest(j)
         part = piece(j, size)
@@ -1131,6 +1134,8 @@
         dkv = v.dkv[span]
         _, _, cosine, sine = tables(first)
         v.dqkv[span, 128:] = (dkv * cosine - half_turn_tile(dkv) * sine).astype(bf16)
+
+    y_scatter.fold_late(0)
 
     o = v.o_own[...].reshape(length, 128)
     dqkv = v.dqkv[...]
@@ -1239,7 +1244,7 @@
         rows_copy(k).wait_send()
     for l in range(local):
         ge_plane.drain(l)
-    for item in (x_line, wo_line, y_scatter, h_scatter):
+    for item in (x_line, wo_line, wo_plane, y_scatter, h_scatter):
         item.drain(0)
     for j in range(PARTS):
         up_line.drain(j)
@@ -1257,9 +1262,41 @@
         out_specs=[anywhere if n == 3 else vmem for n in range(len(outs))],
         scratch_shapes=layer_scratch(rows, local),
         compiler_params=pltpu.CompilerParams(
-            collective_id=0, has_side_effects=True, vmem_limit_bytes=64 * 2**20 - 2**18
+            collective_id=0, has_side_effects=True, vmem_limit_bytes=63 * 2**20 + 2**19
         ),
         name="layer",
+    )(*args)
+
+
+def small_kernel(clip, rates, gn, block_in, grad_in, wa, ma, va, ga, wg, mg, vg, block, grad, *outs):
+    c, one, two = clip[...], rates[:1, :1], rates[:1, 1:2]
+
+    def update(refs, gradient, decay, rate, results):
+        w, g = refs[0][...], gradient * c
+        first = BETA_ONE * refs[1][...] + (1.0 - BETA_ONE) * g
+        second = BETA_TWO * refs[2][...] + (1.0 - BETA_TWO) * g * g
+        step = (first * one) / (jnp.sqrt(second * two) + ADAM_EPSILON)
+        results[0][...] = w - rate * (step + decay * w)
+        results[1][...] = first
+        results[2][...] = second
+
+    update((wa, ma, va), ga[...], WEIGHT_DECAY, LEARN_RATE, outs[:3])
+    update((wg, mg, vg), gn[: wg.shape[0], : wg.shape[1]], 0.0, GAIN_RATE, outs[3:])
+    block[...] = block_in[...]
+    grad[...] = grad_in[...]
+
+
+def call_small(clip, rates, gn, block, grad, attn, ga, gains):
+    vmem = pl.BlockSpec(memory_space=pltpu.VMEM)
+    outs = [jax.ShapeDtypeStruct(a.shape, a.dtype) for a in (block, grad, *attn, *gains)]
+    args = (clip, rates, gn, block, grad, *attn, ga, *gains)
+    return pl.pallas_call(
+        small_kernel,
+        out_shape=outs,
+        in_specs=[vmem] * len(args),
+        out_specs=[vmem] * len(outs),
+        compiler_params=pltpu.CompilerParams(vmem_limit_bytes=63 * 2**20 + 2**19),
+        name="small",
     )(*args)
 
 
@@ -1287,12 +1324,12 @@
     )
     grad_norm = norm.reshape(())
     steps = step_count.astype(jnp.float32)
-    attn = adam_update(
-        w_attn, first_attn, second_attn, grad_attn * clip, steps, WEIGHT_DECAY, LEARN_RATE
-    )
-    gain = adam_update(
-        norm_gains.T, first_gains.T, second_gains.T, gn[:2, : norm_gains.shape[0]] * clip, steps, 0.0, GAIN_RATE
-    )
+    rates = 1.0 / (1.0 - jnp.stack([BETA_ONE**steps, BETA_TWO**steps]))[None]
+    block, input_total, *small = call_small(
+        clip, rates, gn, block, input_total,
+        (w_attn, first_attn, second_attn), grad_attn, (norm_gains.T, first_gains.T, second_gains.T),
+    )
+    attn, gain = small[:3], small[3:]
     expert = adam_update(
         w_expert, first_expert, second_expert, grad_expert * clip[None], steps, WEIGHT_DECAY, LEARN_RATE
     )

time: 194 us -> 191 us (0.985)
  other arithmetic: 13 us -> 9.51 us
  Pallas kernels: 176 us -> 178 us
    pallas_call x0 -> x1, Pallas kernels: none -> 3.76 us  [call_small(): pl.pallas_call(small_kernel, out_shape=outs, in_specs=[vmem] * len(args),...]
    transpose x1 -> x0, other arithmetic: 2.02 us -> none  [fast_body(): return (block[None], input_total[None], grad_norm, *attn, *[a.T for a in...]
    sub x2 -> x1, other arithmetic: 10.9 us -> 8.92 us  [adam_update(): weight - step_rate * (first_hat / (jnp.sqrt(second_hat) + ADAM_EPSILON) +...]
    pallas_call x1, Pallas kernels: 176 us -> 174 us  [call_layer(): pl.pallas_call(layer_kernel, out_shape=outs, in_specs=[anywhere if n == 3...]
where the time goes in v4:
time: 191 us
  Pallas kernels  178 us (93%)
  other arithmetic  9.51 us (5%)
  between operations  3.09 us (2%)
    pallas_call x1, Pallas kernels, call_layer(): pl.pallas_call(layer_kernel, out_shape=outs, in_specs=[anywhere if n == 3...  174 us
    sub x1, other arithmetic, adam_update(): weight - step_rate * (first_hat / (jnp.sqrt(second_hat) + ADAM_EPSILON) +...  8.92 us

profile of v4, /device:TPU:24, one launch (start us, length us, event | category | flops | bytes accessed | tf_op | source)
XLA Modules:
  0.0 190.5 jit_solution(6844159142400518736)
XLA Ops:
  1.4 0.6 fusion.1.rates
  2.0 174.2 %layer.1 = (bf16[128,1024]{1,0:T(8,128)(2,1)}, f32[128,1024]{1,0:T(8,128)}, f32[1,1]{1,0:T(1,128)}, f32[2,256,1536]{2,1,0:T(8,128)}, f32[32,3072]{1,0:T(8,128)}, /*index=5*/f32[8,128]{1,0:T(8,128)}, f32[1,1]{1,0:T(1,128)}) custom-call(bf16[128,1024]{1,0:T(8,128)(2,1)} %bitcast.20, bf16[128,1024]{1,0:T(8,128)(2,1)} %bitcast.21, f32[32,3072]{1,0:T(8,128)} %wa.3, ...), custom_call_target="tpu_custom_call" | custom-call | tf_op jit(solution)/shard_map/layer/pallas_call | solution.py:1258
  176.2 3.8 %small.1 = (bf16[128,1024]{1,0:T(8,128)(2,1)}, f32[128,1024]{1,0:T(8,128)}, f32[32,3072]{1,0:T(8,128)}, f32[32,3072]{1,0:T(8,128)}, f32[32,3072]{1,0:T(8,128)}, ...) custom-call(f32[1,1]{1,0:T(1,128)} %get-tuple-element.27.clip, f32[1,2]{1,0:T(1,128)} %fusion.1.rates, ...), custom_call_target="tpu_custom_call" | custom-call | tf_op jit(solution)/shard_map/small/pallas_call | solution.py:1293
  179.9 8.9 %multiply_subtract_fusion = (f32[2,256,1536]{2,1,0:T(8,128)}, f32[2,256,1536]{2,1,0:T(8,128)}, f32[2,256,1536]{2,1,0:T(8,128)}) fusion(f32[2,256,1536]{2,1,0:T(8,128)} %we.1, f32[]{:T(128)S(6)} %sub.21, f32[]{:T(128)S(6)} %sub.20, f32[2,256,1536]{2,1,0:T(8,128)} %get-tuple-element.41, f32[]{:T(128)} %bitcast.17, f32[2,256,1536]{2,1,0:T(8,128)} %param.31, ...), kind=kLoop, calls=%fused_computation.2 | loop fusion | flops 12582912 | bytes 22020108 | tf_op jit(solution)/shard_map/sub | solution.py:63

commit v5 on v4

--- a/solution.py
+++ b/solution.py
@@ -1042,6 +1042,14 @@
         ge_plane.start(l, chunk)
 
     def second_round(j, carry):
+        @pl.when((j > 0) & (j <= PARTS))
+        def _():
+            d_scatter.fold(j - 1)
+
+        @pl.when(j > 1)
+        def _():
+            d_scatter.fold_late(j - 2)
+
         @pl.when(j < PARTS)
         def _():
             expert(1, j)
@@ -1053,14 +1061,6 @@
 
         for chunk in range(3):
             pl.when(j == chunk)(lambda chunk=chunk: send_chunk(0, chunk))
-
-        @pl.when((j > 0) & (j <= PARTS))
-        def _():
-            d_scatter.fold(j - 1)
-
-        @pl.when(j > 1)
-        def _():
-            d_scatter.fold_late(j - 2)
 
         return carry
 

time: 191 us -> 190 us (level)
  no operation moved by 1% of the time
where the time goes in v5:
time: 190 us
  Pallas kernels  177 us (93%)
  other arithmetic  9.51 us (5%)
  between operations  3.09 us (2%)
    pallas_call x1, Pallas kernels, call_layer(): pl.pallas_call(layer_kernel, out_shape=outs, in_specs=[anywhere if n == 3...  173 us
    sub x1, other arithmetic, adam_update(): weight - step_rate * (first_hat / (jnp.sqrt(second_hat) + ADAM_EPSILON) +...  8.92 us

profile of v5, /device:TPU:24, one launch (start us, length us, event | category | flops | bytes accessed | tf_op | source)
XLA Modules:
  0.0 189.8 jit_solution(17111067815352721564)
XLA Ops:
  1.4 0.6 fusion.1.rates
  2.0 173.5 %layer.1 = (bf16[128,1024]{1,0:T(8,128)(2,1)}, f32[128,1024]{1,0:T(8,128)}, f32[1,1]{1,0:T(1,128)}, f32[2,256,1536]{2,1,0:T(8,128)}, f32[32,3072]{1,0:T(8,128)}, /*index=5*/f32[8,128]{1,0:T(8,128)}, f32[1,1]{1,0:T(1,128)}) custom-call(bf16[128,1024]{1,0:T(8,128)(2,1)} %bitcast.20, bf16[128,1024]{1,0:T(8,128)(2,1)} %bitcast.21, f32[32,3072]{1,0:T(8,128)} %wa.3, ...), custom_call_target="tpu_custom_call" | custom-call | tf_op jit(solution)/shard_map/layer/pallas_call | solution.py:1258
  175.4 3.8 %small.1 = (bf16[128,1024]{1,0:T(8,128)(2,1)}, f32[128,1024]{1,0:T(8,128)}, f32[32,3072]{1,0:T(8,128)}, f32[32,3072]{1,0:T(8,128)}, f32[32,3072]{1,0:T(8,128)}, ...) custom-call(f32[1,1]{1,0:T(1,128)} %get-tuple-element.27.clip, f32[1,2]{1,0:T(1,128)} %fusion.1.rates, ...), custom_call_target="tpu_custom_call" | custom-call | tf_op jit(solution)/shard_map/small/pallas_call | solution.py:1293
  179.2 8.9 %multiply_subtract_fusion = (f32[2,256,1536]{2,1,0:T(8,128)}, f32[2,256,1536]{2,1,0:T(8,128)}, f32[2,256,1536]{2,1,0:T(8,128)}) fusion(f32[2,256,1536]{2,1,0:T(8,128)} %we.1, f32[]{:T(128)S(6)} %sub.21, f32[]{:T(128)S(6)} %sub.20, f32[2,256,1536]{2,1,0:T(8,128)} %get-tuple-element.41, f32[]{:T(128)} %bitcast.17, f32[2,256,1536]{2,1,0:T(8,128)} %param.31, ...), kind=kLoop, calls=%fused_computation.2 | loop fusion | flops 12582912 | bytes 22020108 | tf_op jit(solution)/shard_map/sub | solution.py:63

commit v6 on v5

--- a/solution.py
+++ b/solution.py
@@ -990,13 +990,15 @@
         dgu = jnp.where(routed, jnp.concatenate([dg, du], axis=1), 0.0).astype(bf16)
         v.dgu[l, :, part] = dgu.reshape(SPAN, size, 2 * FF)
         d = dot(dgu, weights[:, : 2 * FF], NT).astype(bf16)
+        if l > 0:
+            summed = v.d[:, part].reshape(-1, D).astype(f32) + d.astype(f32)
+            v.d[:, part] = summed.astype(bf16).reshape(SPAN, size, D)
+            d_scatter.start(j)
         y = dot(act, weights[:, 2 * FF :], NT).astype(bf16)
         if l == 0:
             v.d[:, part] = d.reshape(SPAN, size, D)
             v.o_all[:, part] = y.reshape(SPAN, size, D)
         else:
-            d = v.d[:, part].reshape(-1, D).astype(f32) + d.astype(f32)
-            v.d[:, part] = d.astype(bf16).reshape(SPAN, size, D)
             y = gate_of(0, part) * v.o_all[:, part].reshape(-1, D).astype(f32) + gate * y.astype(f32)
             v.o_all[:, part] = y.astype(bf16).reshape(SPAN, size, D)
 
@@ -1053,7 +1055,6 @@
         @pl.when(j < PARTS)
         def _():
             expert(1, j)
-            d_scatter.start(j)
 
         @pl.when(j == 0)
         def _():
@@ -1084,8 +1085,8 @@
         v.da_all[e, part] = dr.astype(bf16)
         da_line.start(j)
 
+    second_back(0)
     send_chunk(1, 0)
-    second_back(0)
     ge_plane.combine(0)
     send_chunk(1, 1)
     second_back(1)

time: 190 us -> 190 us (level)
  no operation moved by 1% of the time
where the time goes in v6:
time: 190 us; the launch traced here: 189 us
  Pallas kernels  177 us (93%)
  other arithmetic  9.51 us (5%)
  between operations  3.09 us (2%)
    pallas_call x1, Pallas kernels, call_layer(): pl.pallas_call(layer_kernel, out_shape=outs, in_specs=[anywhere if n == 3...  173 us
    sub x1, other arithmetic, adam_update(): weight - step_rate * (first_hat / (jnp.sqrt(second_hat) + ADAM_EPSILON) +...  8.92 us

profile of v6, /device:TPU:24, one launch (start us, length us, event | category | flops | bytes accessed | tf_op | source)
XLA Modules:
  0.0 189.2 jit_solution(6520923362011632323)
XLA Ops:
  1.4 0.6 fusion.1.rates
  2.0 172.9 %layer.1 = (bf16[128,1024]{1,0:T(8,128)(2,1)}, f32[128,1024]{1,0:T(8,128)}, f32[1,1]{1,0:T(1,128)}, f32[2,256,1536]{2,1,0:T(8,128)}, f32[32,3072]{1,0:T(8,128)}, /*index=5*/f32[8,128]{1,0:T(8,128)}, f32[1,1]{1,0:T(1,128)}) custom-call(bf16[128,1024]{1,0:T(8,128)(2,1)} %bitcast.20, bf16[128,1024]{1,0:T(8,128)(2,1)} %bitcast.21, f32[32,3072]{1,0:T(8,128)} %wa.3, ...), custom_call_target="tpu_custom_call" | custom-call | tf_op jit(solution)/shard_map/layer/pallas_call | solution.py:1259
  174.9 3.8 %small.1 = (bf16[128,1024]{1,0:T(8,128)(2,1)}, f32[128,1024]{1,0:T(8,128)}, f32[32,3072]{1,0:T(8,128)}, f32[32,3072]{1,0:T(8,128)}, f32[32,3072]{1,0:T(8,128)}, ...) custom-call(f32[1,1]{1,0:T(1,128)} %get-tuple-element.27.clip, f32[1,2]{1,0:T(1,128)} %fusion.1.rates, ...), custom_call_target="tpu_custom_call" | custom-call | tf_op jit(solution)/shard_map/small/pallas_call | solution.py:1294
  178.6 8.9 %multiply_subtract_fusion = (f32[2,256,1536]{2,1,0:T(8,128)}, f32[2,256,1536]{2,1,0:T(8,128)}, f32[2,256,1536]{2,1,0:T(8,128)}) fusion(f32[2,256,1536]{2,1,0:T(8,128)} %we.1, f32[]{:T(128)S(6)} %sub.21, f32[]{:T(128)S(6)} %sub.20, f32[2,256,1536]{2,1,0:T(8,128)} %get-tuple-element.41, f32[]{:T(128)} %bitcast.17, f32[2,256,1536]{2,1,0:T(8,128)} %param.31, ...), kind=kLoop, calls=%fused_computation.2 | loop fusion | flops 12582912 | bytes 22020108 | tf_op jit(solution)/shard_map/sub | solution.py:63
